TPU v7x, 256 devices: a whole 4x4x8 slice. The times are simulated.
256 devices in a mesh: sub: 32 (over y, x, core), grp: 8 (over z).
Axes of the slice: x: 4, y: 4, z: 8, core: 2. Of those that a mesh axis runs over, the one named last changes fastest.
Arguments:
- residual: bfloat16 [8, 32, 1024, 512], P('grp', 'sub'), may hold values from -6 to 6
- face_order: int32 [8, 32, 1024], P('grp', 'sub'), may hold values from 0 to 1023, each once within a row
- stiffness: float32 [8, 32], replicated, may hold values from 1 to 100
- schur: bfloat16 [8, 32, 1024, 1024], P('grp', 'sub')
- local_inverse: bfloat16 [8, 32, 1024, 1024], P('grp', 'sub')
- coarse_basis: bfloat16 [8, 32, 1024, 128], P('grp', 'sub'), may hold values from -0.1875 to 0.1875
- coarse_map: int32 [8, 32, 128], P('grp', 'sub'), may hold values from 0 to 511, as said below
- level2_inverse: float32 [8, 512, 512], P('grp')
- level2_basis: float32 [8, 512, 128], P('grp'), may hold values from -0.25 to 0.25
- level2_map: int32 [8, 128], P('grp'), may hold values from 0 to 511, as said below
- level3_inverse: float32 [512, 512], replicated
Outputs:
- solution: bfloat16 [8, 32, 1024, 512], P('grp', 'sub')
- image: bfloat16 [8, 32, 1024, 512], P('grp', 'sub')
Inputs may be any that keep to these rules, and one draw needn't show every extreme that they name: `face_order`: each subdomain's row holds every number of 0 to 1023 once. `coarse_map`: within one subdomain the 128 entries are distinct, and each of a group's 512 level-2 coarse values is named by some subdomain of the group. `level2_map`: within one group the 128 entries are distinct, and each level-3 coarse value is named by some group.
All inputs are finite; a program needn't handle non-finite values.
Results may differ from a plain program's by a relative error of at most 0.0062.
Values may be sent and summed in bfloat16 or wider, within the bound.
A program may use at most 64 MiB of HBM per device.

v0:
```python
import jax
import jax.numpy as jnp
from jax import lax
from jax.sharding import PartitionSpec as P

highest = lax.Precision.HIGHEST


def extended(cells, sides, width):
    for axis, dim in sides:
        count = lax.axis_size(axis)
        ends = count - 1
        head = lax.slice_in_dim(cells, 0, width, axis=dim)
        tail = lax.slice_in_dim(cells, cells.shape[dim] - width, cells.shape[dim], axis=dim)
        cells = jnp.concatenate(
            [
                lax.ppermute(tail, axis, [(i, (i + 1) % count) for i in range(ends)]),
                cells,
                lax.ppermute(head, axis, [((i + 1) % count, i) for i in range(ends)]),
            ],
            axis=dim,
        )
    return cells


def face_weights(stiffness, group_index, member_index):
    group_count, member_count = stiffness.shape
    itself = stiffness[group_index, member_index]

    def share_of(other_group, other_member, present):
        neighbour = stiffness[
            jnp.clip(other_group, 0, group_count - 1), jnp.clip(other_member, 0, member_count - 1)
        ]
        return jnp.where(present, itself / (itself + neighbour), jnp.float32(1.0))

    return jnp.stack(
        [
            share_of(group_index, member_index - 1, member_index > 0),
            share_of(group_index, member_index + 1, member_index < member_count - 1),
            share_of(group_index - 1, member_index, group_index > 0),
            share_of(group_index + 1, member_index, group_index < group_count - 1),
        ]
    )


def shards(
    residual,
    face_order,
    stiffness,
    schur,
    local_inverse,
    coarse_basis,
    coarse_map,
    level2_inverse,
    level2_basis,
    level2_map,
    level3_inverse,
):
    resid_block = residual[0, 0]
    interface_size, columns = resid_block.shape
    face_size = interface_size // 4
    ordering = face_order[0, 0]
    inverse = jnp.argsort(ordering)
    group_index = lax.axis_index("grp")
    member_index = lax.axis_index("sub")
    weights = face_weights(stiffness, group_index, member_index)
    face_of = inverse // face_size
    dof_weight = jnp.sum(
        jnp.where(face_of[:, None] == jnp.arange(4)[None, :], weights[None, :], jnp.float32(0.0)),
        axis=1,
    )
    weighted = (dof_weight[:, None] * resid_block.astype(jnp.float32)).astype(jnp.bfloat16)
    contract_rows = (((0,), (0,)), ((), ()))
    coarse_base = coarse_basis[0, 0]
    coarse_res = lax.dot_general(
        coarse_base, weighted, contract_rows, preferred_element_type=jnp.float32
    )
    level2_size = level2_inverse.shape[1]
    local_map = coarse_map[0, 0]
    selector = (local_map[None, :] == jnp.arange(level2_size)[:, None]).astype(jnp.float32)
    contribution = jnp.dot(selector, coarse_res, precision=highest)
    group_base = level2_basis[0]
    group_map = level2_map[0]
    level3_size = level3_inverse.shape[0]
    selector_three = (group_map[None, :] == jnp.arange(level3_size)[:, None]).astype(jnp.float32)
    local_part = jnp.dot(local_inverse[0, 0], weighted, preferred_element_type=jnp.float32)
    group_inverse = level2_inverse[0]
    level2_res = lax.psum(contribution, "sub")
    group_terms = lax.dot_general(group_base, level2_res, contract_rows, precision=highest)
    level3_res = lax.psum(jnp.dot(selector_three, group_terms, precision=highest), "grp")
    level2_local = jnp.dot(group_inverse, level2_res, precision=highest)
    level3_sol = jnp.dot(level3_inverse, level3_res, precision=highest)
    level2_sol = level2_local + jnp.dot(group_base, level3_sol[group_map], precision=highest)
    coarse_part = jnp.dot(coarse_base.astype(jnp.float32), level2_sol[local_map], precision=highest)
    sendable = (dof_weight[:, None] * (local_part + coarse_part)).astype(jnp.bfloat16)
    face_blocks = sendable[ordering].reshape(4, face_size, columns)
    sub_padded = extended(face_blocks[0:2], (("sub", 0),), 1)
    grp_padded = extended(face_blocks[2:4], (("grp", 0),), 1)
    received = jnp.stack([sub_padded[0], sub_padded[3], grp_padded[0], grp_padded[3]])
    summed = (face_blocks.astype(jnp.float32) + received.astype(jnp.float32)).astype(jnp.bfloat16)
    solution = summed.reshape(interface_size, columns)[inverse]
    image = jnp.dot(schur[0, 0], solution, preferred_element_type=jnp.float32).astype(jnp.bfloat16)
    return (solution[None, None], image[None, None])


def solution(mesh):
    placed = (
        P("grp", "sub", None, None),
        P("grp", "sub", None),
        P(),
        P("grp", "sub", None, None),
        P("grp", "sub", None, None),
        P("grp", "sub", None, None),
        P("grp", "sub", None),
        P("grp", None, None),
        P("grp", None, None),
        P("grp", None),
        P(),
    )
    return jax.shard_map(
        shards,
        mesh=mesh,
        in_specs=placed,
        out_specs=(P("grp", "sub", None, None), P("grp", "sub", None, None)),
        check_vma=False,
    )
```

profile of v0, /device:TPU:1, one launch (start us, length us, event | category | flops | bytes accessed | tf_op | source)
XLA Modules:
  0.0 289.0 jit_solution(15084661443975097650)
XLA Ops:
  7.2 0.0 copy-start
  7.2 0.0 all-reduce.3.cloned.1.call-start
  7.2 1.6 fusion.33
  16.3 5.1 %sort.17 = (s32[1024]{0:T(1024)}, s32[1024]{0:T(1024)S(1)}) sort(s32[1024]{0:T(1024)} %bitcast.82, s32[1024]{0:T(1024)S(1)} %iota.13), dimensions={0}, to_apply=%region_0.0 | sort | flops 10240 | bytes 16384 | tf_op jit(solution)/shard_map/jit(argsort)/sort | solution.py:63
  21.4 0.0 copy-start.6
  21.4 0.1 pad_maximum_fusion.1
  21.5 0.1 select_reduce_fusion
  21.6 1.9 fusion.15
  23.6 2.2 fusion.24
  25.8 0.0 all-reduce.3.cloned.1.call-update
  25.8 0.0 copy-start.7
  25.8 0.0 copy-start.5
  25.8 0.0 all-reduce.5.cloned.1.call-start
  25.9 0.0 copy-done.6
  25.9 118.8 %all-reduce.3.cloned.1.call-done = f32[512,512]{1,0:T(8,128)} async-done(((f32[512,512]{1,0:T(8,128)}), f32[512,512]{1,0:T(8,128)}) %all-reduce.3.cloned.1.call-update) | async-done | bytes 1048592 | tf_op jit(solution)/shard_map/psum | solution.py:88
  144.7 3.0 %fusion.20 = f32[512,128]{1,0:T(8,128)S(1)} fusion(f32[512,512]{1,0:T(8,128)} %all-reduce.3.cloned.1.call-done, f32[1,512,128]{2,1,0:T(8,128)S(1)} %copy-done.4), kind=kOutput, calls=%fused_computation.28 | convolution fusion | flops 402653184 | bytes 1572864 | tf_op jit(solution)/shard_map/dot_general | solution.py:89
  147.7 1.6 fusion.25
  149.3 0.0 all-reduce.5.cloned.1.call-update
  149.4 0.0 copy-start.3
  149.4 4.2 %fusion.3 = f32[512,1024]{1,0:T(8,128)} fusion(bf16[1,1,1024,1024]{3,2,1,0:T(8,128)(2,1)S(1)} %copy-done, bf16[1,1,1024,512]{3,2,1,0:T(8,128)(2,1)} %param.11, f32[1024]{0:T(1024)S(1)} %select_reduce_fusion), kind=kOutput, calls=%fused_computation.8 | convolution fusion | flops 1075314688 | bytes 5246976 | tf_op jit(solution)/shard_map/dot_general | solution.py:86
  153.6 67.5 %all-reduce.5.cloned.1.call-done = f32[512,512]{1,0:T(8,128)} async-done(((f32[512,512]{1,0:T(8,128)}), f32[512,512]{1,0:T(8,128)}) %all-reduce.5.cloned.1.call-update) | async-done | bytes 1048592 | tf_op jit(solution)/shard_map/psum | solution.py:90
  221.1 0.0 copy-done.3
  221.1 5.7 %convolution_bitcast_fusion = f32[512,512]{0,1:T(8,128)} fusion(f32[512,512]{1,0:T(8,128)} %all-reduce.5.cloned.1.call-done, f32[512,512]{1,0:T(8,128)S(1)} %copy-done.3), kind=kOutput, calls=%fused_computation.15 | convolution fusion | flops 1610612736 | bytes 3145728 | tf_op jit(solution)/shard_map/dot_general | solution.py:92
  226.8 1.6 copy.17
  228.4 0.8 gather_fusion
  229.1 2.1 fusion.18
  231.2 0.0 copy-done.2
  231.2 5.7 %fusion.12 = f32[512,512]{0,1:T(8,128)} fusion(f32[512,512]{1,0:T(8,128)S(1)} %fusion.18, f32[512,512]{1,0:T(8,128)S(1)} %copy-done.2, f32[1,512,512]{2,1,0:T(8,128)} %param.18), kind=kOutput, calls=%fused_computation.17 | convolution fusion | flops 1610874880 | bytes 4194304 | tf_op jit(solution)/shard_map/dot_general | solution.py:91
  236.9 1.7 copy.18
  238.6 0.8 gather_fusion.1
  239.4 3.7 %fusion.11 = bf16[1024,512]{0,1:T(8,128)(2,1)} fusion(f32[512,1024]{1,0:T(8,128)} %fusion.3, f32[128,512]{1,0:T(8,128)S(1)} %gather_fusion.1, f32[1024]{0:T(1024)S(1)} %select_reduce_fusion, bf16[1,1,1024,128]{3,2,1,0:T(8,128)(2,1)} %param.16), kind=kOutput, calls=%fused_computation.14 | convolution fusion | flops 806879232 | bytes 3674112 | tf_op jit(solution)/shard_map/dot_general | solution.py:94
  243.1 1.5 copy.19
  244.6 5.1 %gather_fusion.2 = bf16[1024,512]{1,0:T(8,128)(2,1)} fusion(bf16[1024,512]{1,0:T(8,128)(2,1)S(1)} %copy.19, s32[1024]{0:T(1024)S(1)} %broadcast_clamp_fusion), kind=kCustom, calls=%fused_computation.2 | custom fusion | bytes 2101248 | tf_op jit(solution)/shard_map/gather | solution.py:96
  249.7 1.3 slice_bitcast_fusion.3
  251.1 7.8 %collective-permute-start = (bf16[1,256,512]{2,1,0:T(8,128)(2,1)S(1)}, bf16[1,256,512]{2,1,0:T(8,128)(2,1)S(1)}, u32[]{:S(2)}, u32[]{:S(2)}) collective-permute-start(bf16[1,256,512]{2,1,0:T(8,128)(2,1)S(1)} %get-tuple-element.10), channel_id=1, source_target_pairs={{0,8},{8,16},{16,24},{24,32},{32,40},{40,48},{48,56},{56,64},{64,7... | collective-permute-start | bytes 786440 | tf_op jit(solution)/shard_map/ppermute | solution.py:17
  258.8 1.9 collective-permute-start.1
  260.7 2.9 collective-permute-start.2
  263.6 1.3 collective-permute-start.3
  264.9 0.0 collective-permute-done
  264.9 1.9 collective-permute-done.1
  266.8 1.1 collective-permute-done.2
  267.9 4.1 %collective-permute-done.3 = bf16[1,256,512]{2,1,0:T(8,128)(2,1)S(1)} collective-permute-done((bf16[1,256,512]{2,1,0:T(8,128)(2,1)S(1)}, bf16[1,256,512]{2,1,0:T(8,128)(2,1)S(1)}, u32[]{:S(2)}, u32[]{:S(2)}) %collective-permute-start.3) | collective-permute-done | bytes 262176 | tf_op jit(solution)/shard_map/ppermute | solution.py:19
  272.0 0.1 pad_maximum_fusion
  272.1 0.0 copy-done.1
  272.1 0.4 fusion
  272.5 5.1 %gather_fusion.3 = bf16[1024,512]{1,0:T(8,128)(2,1)} fusion(bf16[1024,512]{1,0:T(8,128)(2,1)S(1)} %fusion, s32[1024]{0:T(1024)S(1)} %get-tuple-element.14), kind=kCustom, calls=%fused_computation.3 | custom fusion | bytes 2101248 | tf_op jit(solution)/shard_map/gather | solution.py:101
  277.6 3.2 %fusion.8 = bf16[1,1,1024,512]{2,3,1,0:T(8,128)(2,1)S(1)} fusion(bf16[1024,512]{1,0:T(8,128)(2,1)} %gather_fusion.3, bf16[1,1,1024,1024]{3,2,1,0:T(8,128)(2,1)} %param.14), kind=kOutput, calls=%fused_computation.13 | convolution fusion | flops 1074266112 | bytes 4194304 | tf_op jit(solution)/shard_map/dot_general | solution.py:102
  280.8 1.3 copy.20
  (15 shorter events, 0.1 us)
Async XLA Ops:
  7.2 142.2 %copy-start = (bf16[1,1,1024,1024]{3,2,1,0:T(8,128)(2,1)S(1)}, bf16[1,1,1024,1024]{3,2,1,0:T(8,128)(2,1)}, u32[]{:S(2)}) copy-start(bf16[1,1,1024,1024]{3,2,1,0:T(8,128)(2,1)} %param.15) | copy-start | bytes 6291460
  7.2 137.5 %all-reduce.3.cloned.1.call-start = ((), (), s32[]{:S(2)}) async-start(), calls=%async_computation | async-start | bytes 2097152 | tf_op jit(solution)/shard_map/psum | solution.py:88
  21.4 4.5 %copy-start.6 = (s32[1,128]{1,0:T(1,128)S(1)}, s32[1,128]{1,0:T(1,128)}, u32[]{:S(2)}) copy-start(s32[1,128]{1,0:T(1,128)} %param.20) | copy-start | bytes 1540
  21.5 123.2 %copy-start.4 = (f32[1,512,128]{2,1,0:T(8,128)S(1)}, f32[1,512,128]{2,1,0:T(8,128)}, u32[]{:S(2)}) copy-start(f32[1,512,128]{2,1,0:T(8,128)} %param.19) | copy-start | bytes 786436
  25.8 123.5 %copy-start.7 = (s32[1,1,128]{2,1,0:T(1,128)S(1)}, s32[1,1,128]{2,1,0:T(1,128)}, u32[]{:S(2)}) copy-start(s32[1,1,128]{2,1,0:T(1,128)} %param.17) | copy-start | bytes 1540
  25.8 123.5 %copy-start.5 = (s32[1,1,1024]{2,1,0:T(1,128)S(1)}, s32[1,1,1024]{2,1,0:T(1,128)}, u32[]{:S(2)}) copy-start(s32[1,1,1024]{2,1,0:T(1,128)} %param.12) | copy-start | bytes 12292
  25.8 195.3 %all-reduce.5.cloned.1.call-start = ((), (), s32[]{:S(2)}) async-start(), calls=%async_computation.1 | async-start | bytes 2097152 | tf_op jit(solution)/shard_map/psum | solution.py:90
  149.4 71.7 %copy-start.3 = (f32[512,512]{1,0:T(8,128)S(1)}, f32[512,512]{1,0:T(8,128)}, u32[]{:S(2)}) copy-start(f32[512,512]{1,0:T(8,128)} %param.21) | copy-start | bytes 3145732
  229.1 2.1 copy-start.2
  249.7 22.4 %copy-start.1 = (bf16[1024,512]{1,0:T(8,128)(2,1)S(1)}, bf16[1024,512]{1,0:T(8,128)(2,1)}, u32[]{:S(2)}) copy-start(bf16[1024,512]{1,0:T(8,128)(2,1)} %gather_fusion.2) | copy-start | bytes 3145732
  251.1 13.9 %collective-permute-start = (bf16[1,256,512]{2,1,0:T(8,128)(2,1)S(1)}, bf16[1,256,512]{2,1,0:T(8,128)(2,1)S(1)}, u32[]{:S(2)}, u32[]{:S(2)}) collective-permute-start(bf16[1,256,512]{2,1,0:T(8,128)(2,1)S(1)} %get-tuple-element.10), channel_id=1, source_target_pairs={{0,8},{8,16},{16,24},{24,32},{32,40},{40,48},{48,56},{56,64},{64,7... | collective-permute-start | bytes 786440 | tf_op jit(solution)/shard_map/ppermute | solution.py:17
  258.8 8.0 %collective-permute-start.1 = (bf16[1,256,512]{2,1,0:T(8,128)(2,1)S(1)}, bf16[1,256,512]{2,1,0:T(8,128)(2,1)S(1)}, u32[]{:S(2)}, u32[]{:S(2)}) collective-permute-start(bf16[1,256,512]{2,1,0:T(8,128)(2,1)S(1)} %get-tuple-element.12), channel_id=1, source_target_pairs={{8,0},{16,8},{24,16},{32,24},{40,32},{48,40},{56,48},{64,56},{72,6... | collective-permute-start | bytes 786440 | tf_op jit(solution)/shard_map/ppermute | solution.py:19
  260.7 7.1 %collective-permute-start.2 = (bf16[1,256,512]{2,1,0:T(8,128)(2,1)S(1)}, bf16[1,256,512]{2,1,0:T(8,128)(2,1)S(1)}, u32[]{:S(2)}, u32[]{:S(2)}) collective-permute-start(bf16[1,256,512]{2,1,0:T(8,128)(2,1)S(1)} %get-tuple-element.11), channel_id=1, source_target_pairs={{0,1},{1,2},{2,3},{3,4},{4,5},{5,6},{6,7},{8,9},{9,10},{10,11},{11... | collective-permute-start | bytes 786440 | tf_op jit(solution)/shard_map/ppermute | solution.py:17
  263.6 8.4 %collective-permute-start.3 = (bf16[1,256,512]{2,1,0:T(8,128)(2,1)S(1)}, bf16[1,256,512]{2,1,0:T(8,128)(2,1)S(1)}, u32[]{:S(2)}, u32[]{:S(2)}) collective-permute-start(bf16[1,256,512]{2,1,0:T(8,128)(2,1)S(1)} %get-tuple-element.13), channel_id=1, source_target_pairs={{1,0},{2,1},{3,2},{4,3},{5,4},{6,5},{7,6},{9,8},{10,9},{11,10},{12... | collective-permute-start | bytes 786440 | tf_op jit(solution)/shard_map/ppermute | solution.py:19
Sparse Core Ops, SparseCore 0:
  25.9 118.7 all-reduce.2
  149.4 71.6 all-reduce.4
where the time goes:
time: 291 us; the launch traced here: 289 us
  waiting for transfers between devices  193 us (66%)
  matrix products  33.3 us (11%)
  between operations  21.9 us (8%)
  local copies, waits for them, and re-layouts  20.7 us (7%)
  starting transfers between devices  13.9 us (5%)
  other arithmetic  5.76 us (2%)
    psum x1, waiting for transfers between devices, shards(): level2_res = lax.psum(contribution, 'sub')  119 us
    psum x1, waiting for transfers between devices, shards(): lax.psum(jnp.dot(selector_three, group_terms, precision=highest), 'grp')  67.5 us
    ppermute x2, starting transfers between devices, extended(): lax.ppermute(tail, axis, [(i, (i + 1) % count) for i in range(ends)])  10.6 us
    ppermute x2, waiting for transfers between devices, extended(): lax.ppermute(head, axis, [((i + 1) % count, i) for i in range(ends)])  5.98 us
  transfers between devices with their start and end apart: 6, of which 5 were waited for; matrix products, arithmetic and copies ran while one was open for 1% of the time, Pallas kernels for 0%

commit v1 on v0

v1 whole, which is shorter than its diff:
```python
import functools

import jax
import jax.numpy as jnp
from jax import lax
from jax.experimental import pallas as pl
from jax.experimental.pallas import tpu as pltpu
from jax.sharding import PartitionSpec as P

MESH = pl.DeviceIdType.MESH
F32 = jnp.float32
BF16 = jnp.bfloat16
LANES = 128


def dot(a, b):
    return jnp.dot(a, b, preferred_element_type=F32)


def dot_t(a, b):
    return lax.dot_general(a, b, (((1,), (1,)), ((), ())), preferred_element_type=F32)


def two_terms(x):
    high = x.astype(BF16)
    low = (x - high.astype(F32)).astype(BF16)
    return jnp.concatenate([high, low], axis=0)


def fold_terms(x):
    half = x.shape[0] // 2
    return x[:half] + x[half:]


def block(index, size):
    return pl.ds(pl.multiple_of(index * size, size), size)


def kernel(
    nsub,
    ngrp,
    resid_h,
    order_h,
    stiff_h,
    schur_h,
    linv_h,
    basis_h,
    cmap_h,
    l2inv_h,
    l2basis_h,
    l2map_h,
    l3inv_h,
    sol_h,
    img_h,
    resid,
    order,
    stiff,
    schur,
    linv,
    basis,
    cmap,
    l2inv,
    l2basis,
    l2map,
    l3inv,
    cmaps,
    l2maps,
    wcol,
    perm_t,
    perm,
    weighted,
    cres_t,
    recv2,
    onehot2,
    b2,
    onehot3,
    q3,
    recv3,
    term3,
    pre,
    back,
    xcoef,
    basis_f,
    local_f,
    schur_p,
    mine,
    theirs,
    sol_acc,
    img_acc,
    sol,
    img,
    in_sem,
    out_sem,
    map2_sem,
    map3_sem,
    a2a_sem,
    z_sem,
    back_sem,
    face_send,
    face_recv,
):
    grp = lax.axis_index("grp")
    sub = lax.axis_index("sub")
    n_if, cols = resid.shape
    face = n_if // 4
    nc1 = basis.shape[1]
    nc2 = l2basis.shape[1]
    ng2 = l2basis.shape[0]
    ng3 = l3inv.shape[0]
    kc = cols // nsub
    half = cols // 2

    loads = [
        pltpu.make_async_copy(src, dst, in_sem.at[i])
        for i, (src, dst) in enumerate(
            [
                (order_h.at[0], order),
                (stiff_h, stiff),
                (cmap_h.at[0], cmap),
                (l2map_h, l2map),
                (resid_h.at[0, 0], resid),
                (basis_h.at[0, 0], basis),
                (l2basis_h.at[0], l2basis),
                (l3inv_h, l3inv),
                (linv_h.at[0, 0], linv),
                (l2inv_h.at[0], l2inv),
                (schur_h.at[0, 0], schur),
            ]
        )
    ]
    for load in loads:
        load.start()
    (ld_order, ld_stiff, ld_cmap, ld_l2map, ld_resid, ld_basis, ld_l2basis, ld_l3inv, ld_linv, ld_l2inv, ld_schur) = loads

    barrier = pltpu.get_barrier_semaphore()

    def greet_sub(j, carry):
        pl.semaphore_signal(barrier, inc=1, device_id={"sub": lax.rem(sub + j, nsub)}, device_id_type=MESH)
        return carry

    def greet_grp(j, carry):
        pl.semaphore_signal(barrier, inc=1, device_id={"grp": lax.rem(grp + j, ngrp)}, device_id_type=MESH)
        return carry

    lax.fori_loop(1, nsub, greet_sub, 0)
    lax.fori_loop(1, ngrp, greet_grp, 0)

    ld_stiff.wait()
    own = stiff[grp, sub]

    def weight(g, s, present):
        other = stiff[jnp.clip(g, 0, ngrp - 1), jnp.clip(s, 0, nsub - 1)]
        num = jnp.full((8, LANES), own, F32)
        den = num + jnp.full((8, LANES), other, F32)
        return jnp.where(jnp.full((8, LANES), present, jnp.int32) > 0, num / den, F32(1.0))

    exists = [sub > 0, sub < nsub - 1, grp > 0, grp < ngrp - 1]
    weights = [
        weight(grp, sub - 1, exists[0].astype(jnp.int32)),
        weight(grp, sub + 1, exists[1].astype(jnp.int32)),
        weight(grp - 1, sub, exists[2].astype(jnp.int32)),
        weight(grp + 1, sub, exists[3].astype(jnp.int32)),
    ]
    for f in range(4):
        high = weights[f].astype(BF16)
        low = (weights[f] - high.astype(F32)).astype(BF16)
        pair = jnp.concatenate([high[0:1], low[0:1]], axis=1)
        wcol[f * face : (f + 1) * face, :] = jnp.broadcast_to(pair, (face, 2 * LANES))

    ld_order.wait()
    ld_basis.wait()
    ld_resid.wait()

    def weigh(r, carry):
        rows = block(r, face)
        ids = lax.broadcasted_iota(jnp.int32, (face, n_if), 0) + r * face
        pt = jnp.where(ids == order[...], F32(1.0), F32(0.0)).astype(BF16)
        perm_t[rows, :] = pt
        both = dot(pt, wcol[...])
        dofw = both[:, :LANES] + both[:, LANES:]
        res = resid[rows, :].astype(F32)
        reps = -(-cols // LANES)
        wide = jnp.concatenate([dofw] * reps, axis=1)[:, :cols]
        weighted[rows, :] = (wide * res).astype(BF16)
        return carry

    lax.fori_loop(0, 4, weigh, 0)
    coarse = dot(basis[...].astype(F32).T.astype(BF16), weighted[...])
    cres_t[...] = coarse.T.astype(BF16)

    ld_cmap.wait()
    ld_l2map.wait()
    cmaps[sub] = jnp.broadcast_to(cmap[...], (8, nc1))
    l2maps[grp] = jnp.broadcast_to(l2map[...], (8, nc2))
    pl.semaphore_wait(barrier, nsub + ngrp - 2)

    def send_map2(j, carry):
        t = lax.rem(sub + j, nsub)
        pltpu.make_async_remote_copy(
            src_ref=cmaps.at[sub],
            dst_ref=cmaps.at[sub],
            send_sem=map2_sem.at[0],
            recv_sem=map2_sem.at[1],
            device_id={"sub": t},
            device_id_type=MESH,
        ).start()
        return carry

    def send_map3(j, carry):
        t = lax.rem(grp + j, ngrp)
        pltpu.make_async_remote_copy(
            src_ref=l2maps.at[grp],
            dst_ref=l2maps.at[grp],
            send_sem=map3_sem.at[0],
            recv_sem=map3_sem.at[1],
            device_id={"grp": t},
            device_id_type=MESH,
        ).start()
        return carry

    def send_a2a(j, carry):
        t = lax.rem(sub + j, nsub)
        pltpu.make_async_remote_copy(
            src_ref=cres_t.at[block(t, kc), :],
            dst_ref=recv2.at[:, block(sub, nc1)],
            send_sem=a2a_sem.at[0],
            recv_sem=a2a_sem.at[1],
            device_id={"sub": t},
            device_id_type=MESH,
        ).start()
        return carry

    lax.fori_loop(1, nsub, send_map2, 0)
    lax.fori_loop(1, nsub, send_a2a, 0)
    lax.fori_loop(1, ngrp, send_map3, 0)
    recv2[:, block(sub, nc1)] = cres_t[block(sub, kc), :]

    def wait_bytes(ref, sem):
        pltpu.make_async_copy(ref, ref, sem).wait()

    wait_bytes(cmaps.at[pl.ds(0, nsub - 1)], map2_sem.at[1])

    def build2(t, carry):
        ids = lax.broadcasted_iota(jnp.int32, (ng2, nc1), 0)
        onehot2[:, block(t, nc1)] = jnp.where(ids == cmaps[t][0:1], F32(1.0), F32(0.0)).astype(BF16)
        return carry

    lax.fori_loop(0, nsub, build2, 0)

    ld_l2basis.wait()
    l2basis_t = l2basis[...].T.astype(BF16)
    wide2 = min(1024, nsub * nc1)

    def gather2(j, carry):
        b2[:, block(j, wide2)] = dot(l2basis_t, onehot2[:, block(j, wide2)]).astype(BF16)
        return carry

    lax.fori_loop(0, nsub * nc1 // wide2, gather2, 0)

    wait_bytes(recv2.at[:, pl.ds(0, (nsub - 1) * nc1)], a2a_sem.at[1])
    term3[...] = dot_t(recv2[...], b2[...])
    recv3[:, block(grp, nc2)] = term3[...]

    def send_z(j, carry):
        t = lax.rem(grp + j, ngrp)
        pltpu.make_async_remote_copy(
            src_ref=term3,
            dst_ref=recv3.at[:, block(grp, nc2)],
            send_sem=z_sem.at[0],
            recv_sem=z_sem.at[1],
            device_id={"grp": t},
            device_id_type=MESH,
        ).start()
        return carry

    lax.fori_loop(1, ngrp, send_z, 0)

    wait_bytes(l2maps.at[pl.ds(0, ngrp - 1)], map3_sem.at[1])

    def build3(t, carry):
        ids = lax.broadcasted_iota(jnp.int32, (ng3, nc2), 0)
        onehot3[:, block(t, nc2)] = jnp.where(ids == l2maps[t][0:1], F32(1.0), F32(0.0)).astype(BF16)
        return carry

    lax.fori_loop(0, ngrp, build3, 0)
    ld_l3inv.wait()
    own3 = onehot3[:, block(grp, nc2)].astype(F32).T.astype(BF16)
    l3rows = dot(own3, l3inv[...].astype(BF16)).astype(BF16)
    q3[...] = dot(l3rows, onehot3[...]).astype(BF16)

    ld_l2inv.wait()
    res2 = dot_t(recv2[...], onehot2[...])
    local2 = fold_terms(dot_t(two_terms(res2), l2inv[...].astype(BF16)))
    local2 = two_terms(local2)

    def spread2(j, carry):
        pre[:, block(j, wide2)] = fold_terms(dot(local2, onehot2[:, block(j, wide2)]))
        return carry

    lax.fori_loop(0, nsub * nc1 // wide2, spread2, 0)

    wait_bytes(recv3.at[:, pl.ds(0, (ngrp - 1) * nc2)], z_sem.at[1])
    picked = two_terms(fold_terms(dot_t(two_terms(recv3[...]), q3[...])))

    def spread3(j, carry):
        here = block(j, wide2)
        back[:, here] = (pre[:, here] + fold_terms(dot(picked, b2[:, here]))).astype(BF16)
        return carry

    lax.fori_loop(0, nsub * nc1 // wide2, spread3, 0)

    def send_back(j, carry):
        t = lax.rem(sub + j, nsub)
        pltpu.make_async_remote_copy(
            src_ref=back.at[:, block(t, nc1)],
            dst_ref=xcoef.at[block(sub, kc), :],
            send_sem=back_sem.at[0],
            recv_sem=back_sem.at[1],
            device_id={"sub": t},
            device_id_type=MESH,
        ).start()
        return carry

    lax.fori_loop(1, nsub, send_back, 0)
    xcoef[block(sub, kc), :] = back[:, block(sub, nc1)]

    order_col = jnp.broadcast_to(order[...].astype(F32), (LANES, n_if)).T.astype(jnp.int32)

    def build_perm(b, carry):
        ids = lax.broadcasted_iota(jnp.int32, (n_if, LANES), 1) + b * LANES
        perm[:, block(b, LANES)] = jnp.where(ids == order_col, F32(1.0), F32(0.0)).astype(BF16)
        return carry

    lax.fori_loop(0, n_if // LANES, build_perm, 0)
    ld_linv.wait()

    def local(r, carry):
        rows = block(r, face)
        p = perm[rows, :]
        basis_f[rows, :] = dot(p, basis[...]).astype(BF16)
        linv_f = dot(p, linv[...]).astype(BF16)
        local_f[rows, :] = dot(linv_f, weighted[...])
        return carry

    lax.fori_loop(0, 4, local, 0)
    ld_schur.wait()

    def permute_schur(r, carry):
        rows = block(r, face)
        schur_p[rows, :] = dot(schur[rows, :], perm_t[...]).astype(BF16)
        return carry

    lax.fori_loop(0, 4, permute_schur, 0)

    wait_bytes(xcoef.at[pl.ds(0, (nsub - 1) * kc), :], back_sem.at[1])

    def face_copy(f, h):
        axis, step = (("sub", -1), ("sub", 1), ("grp", -1), ("grp", 1))[f]
        at = lax.axis_index(axis)
        size = nsub if axis == "sub" else ngrp
        other = jnp.clip(at + step, 0, size - 1)
        facing = (1, 0, 3, 2)[f]
        here = pl.ds(h * half, half)
        return pltpu.make_async_remote_copy(
            src_ref=mine.at[pl.ds(f * face, face), here],
            dst_ref=theirs.at[pl.ds(facing * face, face), here],
            send_sem=face_send.at[f, h],
            recv_sem=face_recv.at[facing, h],
            device_id={axis: other},
            device_id_type=MESH,
        )

    for h in range(2):
        here = slice(h * half, (h + 1) * half)
        for f in (2, 3, 0, 1):
            rows = slice(f * face, (f + 1) * face)
            coarse_f = dot_t(basis_f[rows, :], xcoef[here, :])
            mine[rows, here] = (weights[f][0:1, 0:1] * (local_f[rows, here] + coarse_f)).astype(BF16)

            @pl.when(exists[f])
            def _(f=f, h=h):
                face_copy(f, h).start()

            @pl.when(jnp.logical_not(exists[f]))
            def _(rows=rows, here=here):
                theirs[rows, here] = jnp.zeros((face, half), BF16)

    def arrive(f, h):
        @pl.when(exists[f])
        def _():
            wait_bytes(theirs.at[pl.ds(f * face, face), pl.ds(h * half, half)], face_recv.at[f, h])

    def summed(f, h):
        rows, here = slice(f * face, (f + 1) * face), slice(h * half, (h + 1) * half)
        return (mine[rows, here].astype(F32) + theirs[rows, here].astype(F32)).astype(BF16)

    for h in range(2):
        here = pl.ds(h * half, half)
        arrive(0, h)
        arrive(1, h)
        lower = jnp.concatenate([summed(0, h), summed(1, h)], axis=0)

        def first(r, carry, lower=lower, here=here):
            rows = block(r, face)
            sol_acc[rows, here] = dot(perm_t[rows, 0 : 2 * face], lower)
            img_acc[rows, here] = dot(schur_p[rows, 0 : 2 * face], lower)
            return carry

        lax.fori_loop(0, 4, first, 0)

    stores = []
    for h in range(2):
        here = pl.ds(h * half, half)
        arrive(2, h)
        arrive(3, h)
        upper = jnp.concatenate([summed(2, h), summed(3, h)], axis=0)

        def second(r, carry, upper=upper, here=here):
            rows = block(r, face)
            sol[rows, here] = (sol_acc[rows, here] + dot(perm_t[rows, 2 * face : 4 * face], upper)).astype(BF16)
            img[rows, here] = (img_acc[rows, here] + dot(schur_p[rows, 2 * face : 4 * face], upper)).astype(BF16)
            return carry

        lax.fori_loop(0, 4, second, 0)
        for i, (src, dst) in enumerate([(sol, sol_h), (img, img_h)]):
            store = pltpu.make_async_copy(src.at[:, here], dst.at[0, 0, :, here], out_sem.at[i, h])
            store.start()
            stores.append(store)

    wait_bytes(cmaps.at[pl.ds(0, nsub - 1)], map2_sem.at[0])
    wait_bytes(l2maps.at[pl.ds(0, ngrp - 1)], map3_sem.at[0])
    wait_bytes(cres_t.at[pl.ds(0, (nsub - 1) * kc), :], a2a_sem.at[0])
    wait_bytes(recv3.at[:, pl.ds(0, (ngrp - 1) * nc2)], z_sem.at[0])
    wait_bytes(back.at[:, pl.ds(0, (nsub - 1) * nc1)], back_sem.at[0])
    for f in range(4):

        @pl.when(exists[f])
        def _(f=f):
            for h in range(2):
                wait_bytes(mine.at[pl.ds(f * face, face), pl.ds(h * half, half)], face_send.at[f, h])

    for store in stores:
        store.wait()


def shards(nsub, ngrp, *args):
    resid, order, stiff, schur, linv, basis, cmap, l2inv, l2basis, l2map, l3inv = args
    n_if, cols = resid.shape[2:]
    nc1 = basis.shape[3]
    ng2, nc2 = l2basis.shape[1:]
    ng3 = l3inv.shape[0]
    kc = cols // nsub
    vmem = pltpu.VMEM
    dma = pltpu.SemaphoreType.DMA
    scratch = [
        vmem((n_if, cols), BF16),
        vmem((1, n_if), jnp.int32),
        pltpu.SMEM((ngrp, nsub), F32),
        vmem((n_if, n_if), BF16),
        vmem((n_if, n_if), BF16),
        vmem((n_if, nc1), BF16),
        vmem((1, nc1), jnp.int32),
        vmem((ng2, ng2), F32),
        vmem((ng2, nc2), F32),
        vmem((1, nc2), jnp.int32),
        vmem((ng3, ng3), F32),
        vmem((nsub, 8, nc1), jnp.int32),
        vmem((ngrp, 8, nc2), jnp.int32),
        vmem((n_if, 2 * LANES), BF16),
        vmem((n_if, n_if), BF16),
        vmem((n_if, n_if), BF16),
        vmem((n_if, cols), BF16),
        vmem((cols, nc1), BF16),
        vmem((kc, nsub * nc1), BF16),
        vmem((ng2, nsub * nc1), BF16),
        vmem((nc2, nsub * nc1), BF16),
        vmem((ng3, ngrp * nc2), BF16),
        vmem((nc2, ngrp * nc2), BF16),
        vmem((kc, ngrp * nc2), F32),
        vmem((kc, nc2), F32),
        vmem((kc, nsub * nc1), F32),
        vmem((kc, nsub * nc1), BF16),
        vmem((cols, nc1), BF16),
        vmem((n_if, nc1), BF16),
        vmem((n_if, cols), F32),
        vmem((n_if, n_if), BF16),
        vmem((n_if, cols), BF16),
        vmem((n_if, cols), BF16),
        vmem((n_if, cols), F32),
        vmem((n_if, cols), F32),
        vmem((n_if, cols), BF16),
        vmem((n_if, cols), BF16),
        dma((11,)),
        dma((2, 2)),
        dma((2,)),
        dma((2,)),
        dma((2,)),
        dma((2,)),
        dma((2,)),
        dma((4, 2)),
        dma((4, 2)),
    ]
    flops = 2 * n_if * cols * n_if * 3 + 4 * n_if**3
    out = jax.ShapeDtypeStruct((1, 1, n_if, cols), BF16)
    return pl.pallas_call(
        functools.partial(kernel, nsub, ngrp),
        out_shape=(out, out),
        in_specs=[pl.BlockSpec(memory_space=pl.ANY)] * 11,
        out_specs=(pl.BlockSpec(memory_space=pl.ANY),) * 2,
        scratch_shapes=scratch,
        compiler_params=pltpu.CompilerParams(
            collective_id=0, has_side_effects=True, vmem_limit_bytes=56 * 1024 * 1024
        ),
        cost_estimate=pl.CostEstimate(flops=flops, bytes_accessed=11 << 20, transcendentals=0),
        name="bddc_apply",
    )(*args)


def solution(mesh):
    placed = (
        P("grp", "sub", None, None),
        P("grp", "sub", None),
        P(),
        P("grp", "sub", None, None),
        P("grp", "sub", None, None),
        P("grp", "sub", None, None),
        P("grp", "sub", None),
        P("grp", None, None),
        P("grp", None, None),
        P("grp", None),
        P(),
    )
    return jax.shard_map(
        functools.partial(shards, mesh.shape["sub"], mesh.shape["grp"]),
        mesh=mesh,
        in_specs=placed,
        out_specs=(P("grp", "sub", None, None), P("grp", "sub", None, None)),
        check_vma=False,
    )
```

time: 291 us -> 49.1 us (0.17)
  waiting for transfers between devices: 193 us -> 0 us
  Pallas kernels: 0 us -> 45 us
  matrix products: 33.3 us -> 0 us
  between operations: 21.9 us -> 0.65 us
  local copies, waits for them, and re-layouts: 20.7 us -> 3.32 us
  starting transfers between devices: 13.9 us -> 0 us
  other arithmetic: 5.76 us -> 0 us
    psum x2 -> x0, waiting for transfers between devices: 186 us -> none  [the longest x1 119 us: shards(): level2_res = lax.psum(contribution, 'sub')]
    pallas_call x0 -> x1, Pallas kernels: none -> 45 us  [shards(): pl.pallas_call(functools.partial(kernel, nsub, ngrp), out_shape=(out, out...]
    dot_general x10 -> x0, matrix products: 33.3 us -> none  [the longest x1 5.67 us: shards(): level2_local = jnp.dot(group_inverse, level2_res, precision=highest)]
    ppermute x4 -> x0, starting transfers between devices: 13.8 us -> none  [the longest x2 10.6 us: extended(): lax.ppermute(tail, axis, [(i, (i + 1) % count) for i in range(ends)])]
    gather x4 -> x0, local copies, waits for them, and re-layouts: 11.7 us -> none  [the longest x1 5.08 us: shards(): face_blocks = sendable[ordering].reshape(4, face_size, columns)]
    ppermute x4 -> x0, waiting for transfers between devices: 7.05 us -> none  [the longest x2 5.98 us: extended(): lax.ppermute(head, axis, [((i + 1) % count, i) for i in range(ends)])]
    sort x1 -> x0, other arithmetic: 5.05 us -> none  [shards(): inverse = jnp.argsort(ordering)]
  transfers between devices with their start and end apart: 6 -> 0, of which waited for: 5 -> 0; matrix products, arithmetic and copies ran while one was open for 1% -> 0% of each run, Pallas kernels for 0% -> 0%
where the time goes in v1:
time: 49.1 us; the launch traced here: 48.9 us
  Pallas kernels  45 us (92%)
  local copies, waits for them, and re-layouts  3.32 us (7%)
  between operations  0.65 us (1%)
    pallas_call x1, Pallas kernels, shards(): pl.pallas_call(functools.partial(kernel, nsub, ngrp), out_shape=(out, out...  45 us
    unnamed x4, local copies, waits for them, and re-layouts  3.32 us

profile of v1, /device:TPU:1, one launch (start us, length us, event | category | flops | bytes accessed | tf_op | source)
XLA Modules:
  0.0 48.9 jit_solution(5704627558358294109)
XLA Ops:
  0.6 45.0 %bddc_apply.1 = (bf16[1,1,1024,512]{3,2,1,0:T(8,128)(2,1)}, bf16[1,1,1024,512]{3,2,1,0:T(8,128)(2,1)}) custom-call(bf16[1,1,1024,512]{3,2,1,0:T(8,128)(2,1)} %resid_h.1, s32[1,1,1024]{2,1,0:T(1,128)} %order_h.1, f32[8,32]{1,0:T(8,128)} %stiff_h.1, bf16[1,1,1024,1024]{3,2,1,0:T(8,128)(2,1)} %schur_h.1, bf16[1,1,1024,1024]{3,2,1,0:T(8,128)(2,1)} %linv_h.1, ...), custom_call_target="tpu_custom_call" | custom-call | flops 7516192768 | bytes 11534336 | tf_op jit(solution)/shard_map/bddc_apply/pallas_call | solution.py:505
  45.6 0.0 copy-start
  45.6 2.4 %copy.15 = bf16[1,1,1024,512]{3,2,1,0:T(8,128)(2,1)} copy(bf16[1,1,1024,512]{3,2,1,0:T(8,128)(2,1)} %get-tuple-element.4) | data formatting | bytes 2097152
  48.0 0.0 copy-done
  48.0 1.0 %copy.16 = bf16[1,1,1024,512]{3,2,1,0:T(8,128)(2,1)} copy(bf16[1,1,1024,512]{3,2,1,0:T(8,128)(2,1)S(1)} %copy-done) | data formatting | bytes 2097152
Async XLA Ops:
  45.6 2.4 %copy-start = (bf16[1,1,1024,512]{3,2,1,0:T(8,128)(2,1)S(1)}, bf16[1,1,1024,512]{3,2,1,0:T(8,128)(2,1)}, u32[]{:S(2)}) copy-start(bf16[1,1,1024,512]{3,2,1,0:T(8,128)(2,1)} %get-tuple-element.5) | copy-start | bytes 3145732

commit v2 on v1

v2 whole, which is shorter than its diff:
```python
import functools

import jax
import jax.numpy as jnp
from jax import lax
from jax.experimental import pallas as pl
from jax.experimental.pallas import tpu as pltpu
from jax.sharding import PartitionSpec as P

MESH = pl.DeviceIdType.MESH
F32 = jnp.float32
BF16 = jnp.bfloat16
LANES = 128


def dot(a, b):
    return jnp.dot(a, b, preferred_element_type=F32)


def dot_t(a, b):
    return lax.dot_general(a, b, (((1,), (1,)), ((), ())), preferred_element_type=F32)


def two_terms(x):
    high = x.astype(BF16)
    low = (x - high.astype(F32)).astype(BF16)
    return jnp.concatenate([high, low], axis=0)


def fold_terms(x):
    half = x.shape[0] // 2
    return x[:half] + x[half:]


def block(index, size):
    return pl.ds(pl.multiple_of(index * size, size), size)


def kernel(
    nsub,
    ngrp,
    resid_v,
    order_v,
    stiff_h,
    schur_h,
    linv_h,
    basis_v,
    cmap_v,
    l2inv_h,
    l2basis_h,
    l2map_v,
    l3inv_h,
    sol_v,
    img_v,
    stiff,
    schur,
    linv,
    l2inv,
    l2basis,
    l3inv,
    cmaps,
    l2maps,
    perm_t,
    perm,
    dofw,
    weighted,
    cres_t,
    recv2,
    onehot2,
    b2,
    onehot3,
    q3,
    recv3,
    term3,
    back,
    xcoef,
    local,
    schur_p,
    sendable,
    mine,
    theirs,
    sol_acc,
    img_acc,
    in_sem,
    map2_sem,
    map3_sem,
    a2a_sem,
    z_sem,
    back_sem,
    face_send,
    face_recv,
):
    grp = lax.axis_index("grp")
    sub = lax.axis_index("sub")
    n_if, cols = weighted.shape
    face = n_if // 4
    nc1 = xcoef.shape[1]
    ng2, nc2 = l2basis.shape
    ng3 = l3inv.shape[0]
    kc = cols // nsub
    half = cols // 2
    basis = basis_v[0, 0]
    order = order_v[0]

    loads = [
        pltpu.make_async_copy(src, dst, in_sem.at[i])
        for i, (src, dst) in enumerate(
            [
                (stiff_h, stiff),
                (l2basis_h.at[0], l2basis),
                (l2inv_h.at[0], l2inv),
                (l3inv_h, l3inv),
                (linv_h.at[0, 0], linv),
                (schur_h.at[0, 0], schur),
            ]
        )
    ]
    for load in loads:
        load.start()
    ld_stiff, ld_l2basis, ld_l2inv, ld_l3inv, ld_linv, ld_schur = loads

    barrier = pltpu.get_barrier_semaphore()

    def greet_sub(j, carry):
        pl.semaphore_signal(barrier, inc=1, device_id={"sub": lax.rem(sub + j, nsub)}, device_id_type=MESH)
        return carry

    def greet_grp(j, carry):
        pl.semaphore_signal(barrier, inc=1, device_id={"grp": lax.rem(grp + j, ngrp)}, device_id_type=MESH)
        return carry

    lax.fori_loop(1, nsub, greet_sub, 0)
    lax.fori_loop(1, ngrp, greet_grp, 0)

    cmaps[sub] = jnp.broadcast_to(cmap_v[0], (8, nc1))
    l2maps[grp] = jnp.broadcast_to(l2map_v[...], (8, nc2))
    ld_stiff.wait()
    own = stiff[grp, sub]

    def weight(g, s, present):
        other = stiff[jnp.clip(g, 0, ngrp - 1), jnp.clip(s, 0, nsub - 1)]
        num = jnp.full((8, face), own, F32)
        den = num + jnp.full((8, face), other, F32)
        here = jnp.full((8, face), present.astype(jnp.int32), jnp.int32) > 0
        return jnp.where(here, num / den, F32(1.0))[0:1]

    exists = [sub > 0, sub < nsub - 1, grp > 0, grp < ngrp - 1]
    weights = jnp.concatenate(
        [
            weight(grp, sub - 1, exists[0]),
            weight(grp, sub + 1, exists[1]),
            weight(grp - 1, sub, exists[2]),
            weight(grp + 1, sub, exists[3]),
        ],
        axis=1,
    )

    pl.semaphore_wait(barrier, nsub + ngrp - 2)

    def send_map2(j, carry):
        t = lax.rem(sub + j, nsub)
        pltpu.make_async_remote_copy(
            src_ref=cmaps.at[sub],
            dst_ref=cmaps.at[sub],
            send_sem=map2_sem.at[0],
            recv_sem=map2_sem.at[1],
            device_id={"sub": t},
            device_id_type=MESH,
        ).start()
        return carry

    def send_map3(j, carry):
        t = lax.rem(grp + j, ngrp)
        pltpu.make_async_remote_copy(
            src_ref=l2maps.at[grp],
            dst_ref=l2maps.at[grp],
            send_sem=map3_sem.at[0],
            recv_sem=map3_sem.at[1],
            device_id={"grp": t},
            device_id_type=MESH,
        ).start()
        return carry

    lax.fori_loop(1, nsub, send_map2, 0)
    lax.fori_loop(1, ngrp, send_map3, 0)

    def weigh(r, carry):
        rows = block(r, face)
        ids = lax.broadcasted_iota(jnp.int32, (face, n_if), 0) + r * face
        here = ids == order
        perm_t[rows, :] = jnp.where(here, F32(1.0), F32(0.0)).astype(BF16)
        dw = jnp.sum(jnp.where(here, weights, F32(0.0)), axis=1, keepdims=True)
        dofw[rows, :] = jnp.broadcast_to(dw, (face, LANES))
        weighted[rows, :] = (dw * resid_v[0, 0, rows, :].astype(F32)).astype(BF16)
        return carry

    lax.fori_loop(0, 4, weigh, 0)
    coarse = dot(basis.astype(F32).T.astype(BF16), weighted[...])
    cres_t[...] = coarse.T.astype(BF16)

    def send_a2a(j, carry):
        t = lax.rem(sub + j, nsub)
        pltpu.make_async_remote_copy(
            src_ref=cres_t.at[block(t, kc), :],
            dst_ref=recv2.at[:, block(sub, nc1)],
            send_sem=a2a_sem.at[0],
            recv_sem=a2a_sem.at[1],
            device_id={"sub": t},
            device_id_type=MESH,
        ).start()
        return carry

    lax.fori_loop(1, nsub, send_a2a, 0)
    recv2[:, block(sub, nc1)] = cres_t[block(sub, kc), :]

    def wait_bytes(ref, sem):
        pltpu.make_async_copy(ref, ref, sem).wait()

    wait_bytes(cmaps.at[pl.ds(0, nsub - 1)], map2_sem.at[1])

    def build2(t, carry):
        ids = lax.broadcasted_iota(jnp.int32, (ng2, nc1), 0)
        onehot2[:, block(t, nc1)] = jnp.where(ids == cmaps[t][0:1], F32(1.0), F32(0.0)).astype(BF16)
        return carry

    lax.fori_loop(0, nsub, build2, 0)

    ld_l2basis.wait()
    l2basis_t = l2basis[...].T.astype(BF16)
    wide2 = min(1024, nsub * nc1)

    def gather2(j, carry):
        b2[:, block(j, wide2)] = dot(l2basis_t, onehot2[:, block(j, wide2)]).astype(BF16)
        return carry

    lax.fori_loop(0, nsub * nc1 // wide2, gather2, 0)

    wait_bytes(recv2.at[:, pl.ds(0, (nsub - 1) * nc1)], a2a_sem.at[1])
    term3[...] = dot_t(recv2[...], b2[...])
    recv3[:, block(grp, nc2)] = term3[...]

    def send_z(j, carry):
        t = lax.rem(grp + j, ngrp)
        pltpu.make_async_remote_copy(
            src_ref=term3,
            dst_ref=recv3.at[:, block(grp, nc2)],
            send_sem=z_sem.at[0],
            recv_sem=z_sem.at[1],
            device_id={"grp": t},
            device_id_type=MESH,
        ).start()
        return carry

    lax.fori_loop(1, ngrp, send_z, 0)

    ld_l2inv.wait()
    res2 = dot_t(recv2[...], onehot2[...])
    local2 = fold_terms(dot_t(two_terms(res2), l2inv[...].astype(BF16)))
    wait_bytes(l2maps.at[pl.ds(0, ngrp - 1)], map3_sem.at[1])

    def build3(t, carry):
        ids = lax.broadcasted_iota(jnp.int32, (ng3, nc2), 0)
        onehot3[:, block(t, nc2)] = jnp.where(ids == l2maps[t][0:1], F32(1.0), F32(0.0)).astype(BF16)
        return carry

    lax.fori_loop(0, ngrp, build3, 0)
    ld_l3inv.wait()
    own3 = onehot3[:, block(grp, nc2)].astype(F32).T.astype(BF16)
    l3rows = dot(own3, l3inv[...].astype(BF16)).astype(BF16)
    q3[...] = dot(l3rows, onehot3[...]).astype(BF16)

    wait_bytes(recv3.at[:, pl.ds(0, (ngrp - 1) * nc2)], z_sem.at[1])
    picked = two_terms(fold_terms(dot_t(two_terms(recv3[...]), q3[...])))
    sol2 = (local2 + fold_terms(dot(picked, l2basis_t))).astype(BF16)

    def spread(j, carry):
        back[:, block(j, wide2)] = dot(sol2, onehot2[:, block(j, wide2)]).astype(BF16)
        return carry

    lax.fori_loop(0, nsub * nc1 // wide2, spread, 0)

    def send_back(j, carry):
        t = lax.rem(sub + j, nsub)
        pltpu.make_async_remote_copy(
            src_ref=back.at[:, block(t, nc1)],
            dst_ref=xcoef.at[block(sub, kc), :],
            send_sem=back_sem.at[0],
            recv_sem=back_sem.at[1],
            device_id={"sub": t},
            device_id_type=MESH,
        ).start()
        return carry

    lax.fori_loop(1, nsub, send_back, 0)
    xcoef[block(sub, kc), :] = back[:, block(sub, nc1)]

    ld_linv.wait()
    local[...] = dot(linv[...], weighted[...])
    order_col = jnp.broadcast_to(order.astype(F32), (LANES, n_if)).T.astype(jnp.int32)

    def build_perm(b, carry):
        ids = lax.broadcasted_iota(jnp.int32, (n_if, LANES), 1) + b * LANES
        perm[:, block(b, LANES)] = jnp.where(ids == order_col, F32(1.0), F32(0.0)).astype(BF16)
        return carry

    lax.fori_loop(0, n_if // LANES, build_perm, 0)

    def face_copy(f, h):
        axis, step = (("sub", -1), ("sub", 1), ("grp", -1), ("grp", 1))[f]
        at = lax.axis_index(axis)
        size = nsub if axis == "sub" else ngrp
        other = jnp.clip(at + step, 0, size - 1)
        facing = (1, 0, 3, 2)[f]
        here = pl.ds(h * half, half)
        return pltpu.make_async_remote_copy(
            src_ref=mine.at[pl.ds(f * face, face), here],
            dst_ref=theirs.at[pl.ds(facing * face, face), here],
            send_sem=face_send.at[f, h],
            recv_sem=face_recv.at[facing, h],
            device_id={axis: other},
            device_id_type=MESH,
        )

    wait_bytes(xcoef.at[pl.ds(0, (nsub - 1) * kc), :], back_sem.at[1])

    for h in range(2):
        here = slice(h * half, (h + 1) * half)
        coarse_part = dot_t(basis, xcoef[here, :])
        reps = -(-half // LANES)
        wide = jnp.concatenate([dofw[...]] * reps, axis=1)[:, :half]
        sendable[...] = (wide * (local[:, here] + coarse_part)).astype(BF16)
        for pair in ((2, 3), (0, 1)):
            rows = slice(pair[0] * face, (pair[1] + 1) * face)
            mine[rows, here] = dot(perm[rows, :], sendable[...]).astype(BF16)
            for f in pair:

                @pl.when(exists[f])
                def _(f=f, h=h):
                    face_copy(f, h).start()

                @pl.when(jnp.logical_not(exists[f]))
                def _(f=f, here=here):
                    theirs[f * face : (f + 1) * face, here] = jnp.zeros((face, half), BF16)

    ld_schur.wait()
    wide_p = n_if // 2

    def permute_schur(j, carry):
        schur_p[:, block(j, wide_p)] = dot(schur[...], perm_t[:, block(j, wide_p)]).astype(BF16)
        return carry

    lax.fori_loop(0, n_if // wide_p, permute_schur, 0)

    def arrive(f, h):
        @pl.when(exists[f])
        def _():
            wait_bytes(theirs.at[pl.ds(f * face, face), pl.ds(h * half, half)], face_recv.at[f, h])

    def summed(pair, h):
        rows, here = slice(pair[0] * face, (pair[1] + 1) * face), slice(h * half, (h + 1) * half)
        return (mine[rows, here].astype(F32) + theirs[rows, here].astype(F32)).astype(BF16)

    for h in range(2):
        here = slice(h * half, (h + 1) * half)
        arrive(0, h)
        arrive(1, h)
        lower = summed((0, 1), h)
        sol_acc[:, here] = dot(perm_t[:, 0 : 2 * face], lower).astype(BF16)
        img_acc[:, here] = dot(schur_p[:, 0 : 2 * face], lower)

    for h in range(2):
        here = slice(h * half, (h + 1) * half)
        arrive(2, h)
        arrive(3, h)
        upper = summed((2, 3), h)
        sol_v[0, 0, :, here] = (sol_acc[:, here].astype(F32) + dot(perm_t[:, 2 * face :], upper)).astype(BF16)
        img_v[0, 0, :, here] = (img_acc[:, here] + dot(schur_p[:, 2 * face :], upper)).astype(BF16)

    wait_bytes(cmaps.at[pl.ds(0, nsub - 1)], map2_sem.at[0])
    wait_bytes(l2maps.at[pl.ds(0, ngrp - 1)], map3_sem.at[0])
    wait_bytes(cres_t.at[pl.ds(0, (nsub - 1) * kc), :], a2a_sem.at[0])
    wait_bytes(recv3.at[:, pl.ds(0, (ngrp - 1) * nc2)], z_sem.at[0])
    wait_bytes(back.at[:, pl.ds(0, (nsub - 1) * nc1)], back_sem.at[0])
    for f in range(4):

        @pl.when(exists[f])
        def _(f=f):
            for h in range(2):
                wait_bytes(mine.at[pl.ds(f * face, face), pl.ds(h * half, half)], face_send.at[f, h])


def store(sol, img, sol_h, img_h, sem):
    copies = [pltpu.make_async_copy(sol, sol_h, sem.at[0]), pltpu.make_async_copy(img, img_h, sem.at[1])]
    for copy in copies:
        copy.start()
    for copy in copies:
        copy.wait()


def shards(nsub, ngrp, *args):
    resid, order, stiff, schur, linv, basis, cmap, l2inv, l2basis, l2map, l3inv = args
    n_if, cols = resid.shape[2:]
    nc1 = basis.shape[3]
    ng2, nc2 = l2basis.shape[1:]
    ng3 = l3inv.shape[0]
    kc = cols // nsub
    half = cols // 2
    vmem = pltpu.VMEM
    dma = pltpu.SemaphoreType.DMA
    scratch = [
        pltpu.SMEM((ngrp, nsub), F32),
        vmem((n_if, n_if), BF16),
        vmem((n_if, n_if), BF16),
        vmem((ng2, ng2), F32),
        vmem((ng2, nc2), F32),
        vmem((ng3, ng3), F32),
        vmem((nsub, 8, nc1), jnp.int32),
        vmem((ngrp, 8, nc2), jnp.int32),
        vmem((n_if, n_if), BF16),
        vmem((n_if, n_if), BF16),
        vmem((n_if, LANES), F32),
        vmem((n_if, cols), BF16),
        vmem((cols, nc1), BF16),
        vmem((kc, nsub * nc1), BF16),
        vmem((ng2, nsub * nc1), BF16),
        vmem((nc2, nsub * nc1), BF16),
        vmem((ng3, ngrp * nc2), BF16),
        vmem((nc2, ngrp * nc2), BF16),
        vmem((kc, ngrp * nc2), F32),
        vmem((kc, nc2), F32),
        vmem((kc, nsub * nc1), BF16),
        vmem((cols, nc1), BF16),
        vmem((n_if, cols), F32),
        vmem((n_if, n_if), BF16),
        vmem((n_if, half), BF16),
        vmem((n_if, cols), BF16),
        vmem((n_if, cols), BF16),
        vmem((n_if, cols), BF16),
        vmem((n_if, cols), F32),
        dma((6,)),
        dma((2,)),
        dma((2,)),
        dma((2,)),
        dma((2,)),
        dma((2,)),
        dma((4, 2)),
        dma((4, 2)),
    ]
    flops = 2 * n_if * cols * n_if * 4 + 2 * n_if**3
    out = jax.ShapeDtypeStruct((1, 1, n_if, cols), BF16)
    any_, in_vmem = pl.BlockSpec(memory_space=pl.ANY), pl.BlockSpec(memory_space=vmem)
    done = pl.pallas_call(
        functools.partial(kernel, nsub, ngrp),
        out_shape=(out, out),
        in_specs=[in_vmem, in_vmem, any_, any_, any_, in_vmem, in_vmem, any_, any_, in_vmem, any_],
        out_specs=(in_vmem, in_vmem),
        scratch_shapes=scratch,
        compiler_params=pltpu.CompilerParams(
            collective_id=0, has_side_effects=True, vmem_limit_bytes=50 * 1024 * 1024
        ),
        cost_estimate=pl.CostEstimate(flops=flops, bytes_accessed=11 << 20, transcendentals=0),
        name="bddc_apply",
    )(*args)
    return pl.pallas_call(
        store,
        out_shape=(out, out),
        in_specs=[any_, any_],
        out_specs=(any_, any_),
        scratch_shapes=[dma((2,))],
        name="store",
    )(*done)


def solution(mesh):
    placed = (
        P("grp", "sub", None, None),
        P("grp", "sub", None),
        P(),
        P("grp", "sub", None, None),
        P("grp", "sub", None, None),
        P("grp", "sub", None, None),
        P("grp", "sub", None),
        P("grp", None, None),
        P("grp", None, None),
        P("grp", None),
        P(),
    )
    return jax.shard_map(
        functools.partial(shards, mesh.shape["sub"], mesh.shape["grp"]),
        mesh=mesh,
        in_specs=placed,
        out_specs=(P("grp", "sub", None, None), P("grp", "sub", None, None)),
        check_vma=False,
    )
```

time: 49.1 us -> 114 us (2.32)
  Pallas kernels: 45 us -> 105 us
  local copies, waits for them, and re-layouts: 3.32 us -> 7.78 us
    pallas_call x0 -> x1, Pallas kernels: none -> 64.6 us  [shards(): pl.pallas_call(store, out_shape=(out, out), in_specs=[any_, any_], out_sp...]
    pallas_call x1, Pallas kernels: 45 us -> 40.3 us  [shards(): pl.pallas_call(functools.partial(kernel, nsub, ngrp), out_shape=(out, out...]
    unnamed x4 -> x18, local copies, waits for them, and re-layouts: 3.32 us -> 7.78 us
where the time goes in v2:
time: 114 us; the launch traced here: 113 us
  Pallas kernels  105 us (92%)
  local copies, waits for them, and re-layouts  7.78 us (7%)
    pallas_call x1, Pallas kernels, shards(): pl.pallas_call(store, out_shape=(out, out), in_specs=[any_, any_], out_sp...  64.6 us
    pallas_call x1, Pallas kernels, shards(): pl.pallas_call(functools.partial(kernel, nsub, ngrp), out_shape=(out, out...  40.3 us
    unnamed x18, local copies, waits for them, and re-layouts  7.78 us

profile of v2, /device:TPU:1, one launch (start us, length us, event | category | flops | bytes accessed | tf_op | source)
XLA Modules:
  0.0 113.4 jit_solution(13877123995401342878)
XLA Ops:
  0.6 0.0 copy-start.2
  0.6 1.2 %copy-done.2 = bf16[1,1,1024,512]{3,2,1,0:T(8,128)(2,1)S(1)} copy-done((bf16[1,1,1024,512]{3,2,1,0:T(8,128)(2,1)S(1)}, bf16[1,1,1024,512]{3,2,1,0:T(8,128)(2,1)}, u32[]{:S(2)}) %copy-start.2) | copy-done | bytes 1048600
  1.9 0.0 copy-start.3
  1.9 0.9 copy-done.3
  2.8 0.0 copy-start.4
  2.8 0.9 copy-done.4
  3.8 0.0 copy-start.5
  3.8 0.7 copy-done.5
  4.4 0.0 copy-start.6
  4.5 0.7 copy-done.6
  5.1 0.0 copy-start.7
  5.1 0.7 copy-done.7
  5.8 0.0 copy-start.8
  5.8 0.7 copy-done.8
  6.4 40.3 %bddc_apply.1 = (bf16[1,1,1024,512]{3,2,1,0:T(8,128)(2,1)S(1)}, bf16[1,1,1024,512]{3,2,1,0:T(8,128)(2,1)S(1)}) custom-call(bf16[1,1,1024,512]{3,2,1,0:T(8,128)(2,1)S(1)} %copy-done.2, s32[1,1,1024]{2,1,0:T(1,128)S(1)} %copy-done.5, f32[8,32]{1,0:T(8,128)S(1)} %copy-done.6, bf16[1,1,1024,1024]{3,2,1,0:T(8,128)(2,1)} %schur_h.1, ...), custom_call_target="tpu_custom_call" | custom-call | flops 6442450944 | bytes 11534336 | tf_op jit(solution)/shard_map/bddc_apply/pallas_call | solution.py:452
  46.8 0.0 copy-start
  46.8 1.0 copy-done
  47.7 0.0 copy-start.1
  47.7 1.0 copy-done.1
  48.8 64.6 %store.1 = (bf16[1,1,1024,512]{3,2,1,0:T(8,128)(2,1)}, bf16[1,1,1024,512]{3,2,1,0:T(8,128)(2,1)}) custom-call(bf16[1,1,1024,512]{3,2,1,0:T(8,128)(2,1)} %copy-done, bf16[1,1,1024,512]{3,2,1,0:T(8,128)(2,1)} %copy-done.1), custom_call_target="tpu_custom_call" | custom-call | tf_op jit(solution)/shard_map/store/pallas_call | solution.py:464
Async XLA Ops:
  0.6 1.2 %copy-start.2 = (bf16[1,1,1024,512]{3,2,1,0:T(8,128)(2,1)S(1)}, bf16[1,1,1024,512]{3,2,1,0:T(8,128)(2,1)}, u32[]{:S(2)}) copy-start(bf16[1,1,1024,512]{3,2,1,0:T(8,128)(2,1)} %resid_v.1) | copy-start | bytes 3145732
  1.9 0.9 copy-start.3
  2.8 0.9 copy-start.4
  3.8 0.7 copy-start.5
  4.4 0.7 copy-start.6
  5.1 0.7 copy-start.7
  5.8 0.7 copy-start.8
  46.8 1.0 copy-start
  47.7 1.0 copy-start.1

commit v3 on v2

v3 whole, which is shorter than its diff:
```python
import functools

import jax
import jax.numpy as jnp
from jax import lax
from jax.experimental import pallas as pl
from jax.experimental.pallas import tpu as pltpu
from jax.sharding import PartitionSpec as P

MESH = pl.DeviceIdType.MESH
F32 = jnp.float32
BF16 = jnp.bfloat16
LANES = 128


def dot(a, b):
    return jnp.dot(a, b, preferred_element_type=F32)


def dot_t(a, b):
    return lax.dot_general(a, b, (((1,), (1,)), ((), ())), preferred_element_type=F32)


def two_terms(x):
    high = x.astype(BF16)
    low = (x - high.astype(F32)).astype(BF16)
    return jnp.concatenate([high, low], axis=0)


def fold_terms(x):
    half = x.shape[0] // 2
    return x[:half] + x[half:]


def block(index, size):
    return pl.ds(pl.multiple_of(index * size, size), size)


def far_first(r):
    return r + lax.div(r, 2) - 2 * lax.div(r, 3)


def kernel(
    nsub,
    ngrp,
    resid_h,
    order_h,
    stiff_h,
    schur_h,
    linv_h,
    basis_h,
    cmap_h,
    l2inv_h,
    l2basis_h,
    l2map_h,
    l3inv_h,
    sol_h,
    img_h,
    resid,
    order_s,
    basis_s,
    cmap,
    l2map,
    stiff,
    schur,
    linv,
    l2inv,
    l2basis,
    l3inv,
    l2maps,
    perm_t,
    perm,
    dofw,
    weighted,
    t_src,
    t_recv,
    c_src,
    c_recv,
    recv2,
    onehot2,
    onehot3,
    q3,
    recv3,
    term3,
    back,
    xcoef,
    xn,
    scaled,
    mine_l,
    theirs_l,
    basis_f,
    basis_n,
    schur_p,
    mine,
    sol_acc,
    img_acc,
    sol,
    img,
    in_sem,
    out_sem,
    map3_sem,
    t_sem,
    c_sem,
    z_sem,
    back_sem,
    lf_send,
    lf_recv,
    bf_send,
    bf_recv,
    xf_send,
    xf_recv,
):
    grp = lax.axis_index("grp")
    sub = lax.axis_index("sub")
    n_if, cols = weighted.shape
    face = n_if // 4
    nc1 = xcoef.shape[1]
    ng2, nc2 = l2basis.shape
    ng3 = l3inv.shape[0]
    kc = cols // nsub
    half = cols // 2

    loads = [
        pltpu.make_async_copy(src, dst, in_sem.at[i])
        for i, (src, dst) in enumerate(
            [
                (order_h.at[0], order_s),
                (stiff_h, stiff),
                (cmap_h.at[0], cmap),
                (l2map_h, l2map),
                (resid_h.at[0, 0], resid),
                (basis_h.at[0, 0], basis_s),
                (l2basis_h.at[0], l2basis),
                (linv_h.at[0, 0], linv),
                (l2inv_h.at[0], l2inv),
                (l3inv_h, l3inv),
                (schur_h.at[0, 0], schur),
            ]
        )
    ]
    for load in loads[:8]:
        load.start()
    ld_order, ld_stiff, ld_cmap, ld_l2map, ld_resid, ld_basis, ld_l2basis, ld_linv, ld_l2inv, ld_l3inv, ld_schur = loads

    nx = 4 if nsub % 8 == 0 else 2
    ny = nsub // (2 * nx)
    at_y, at_x, at_c = lax.div(sub, 2 * nx), lax.rem(lax.div(sub, 2), nx), lax.rem(sub, 2)

    def peer_sub(i):
        j = nsub - 1 - i
        y = lax.rem(at_y + far_first(lax.div(j, 2 * nx)), ny)
        x = lax.rem(at_x + far_first(lax.rem(lax.div(j, 2), nx)), nx)
        return (y * nx + x) * 2 + lax.rem(at_c + lax.rem(j, 2), 2)

    def peer_grp(i):
        off = ngrp // 2 + lax.div(i + 1, 2) * (1 - 2 * lax.rem(i, 2))
        return lax.rem(grp + off, ngrp)

    barrier = pltpu.get_barrier_semaphore()

    def greet_sub(i, carry):
        pl.semaphore_signal(barrier, inc=1, device_id={"sub": peer_sub(i)}, device_id_type=MESH)
        return carry

    def greet_grp(i, carry):
        pl.semaphore_signal(barrier, inc=1, device_id={"grp": peer_grp(i)}, device_id_type=MESH)
        return carry

    lax.fori_loop(0, nsub - 1, greet_sub, 0)
    lax.fori_loop(0, ngrp - 1, greet_grp, 0)

    ld_stiff.wait()
    own = stiff[grp, sub]
    exists = [sub > 0, sub < nsub - 1, grp > 0, grp < ngrp - 1]
    weights, their_weights = [], []
    for f, (g, s) in enumerate(((grp, sub - 1), (grp, sub + 1), (grp - 1, sub), (grp + 1, sub))):
        other = stiff[jnp.clip(g, 0, ngrp - 1), jnp.clip(s, 0, nsub - 1)]
        here = jnp.full((8, face), exists[f].astype(jnp.int32), jnp.int32) > 0
        num, nbr = jnp.full((8, face), own, F32), jnp.full((8, face), other, F32)
        weights.append(jnp.where(here, num / (num + nbr), F32(1.0))[0:1])
        their_weights.append((nbr / (nbr + num))[0:1])
    all_weights = jnp.concatenate(weights, axis=1)

    for f in range(4):

        @pl.when(jnp.logical_not(exists[f]))
        def _(f=f):
            rows = slice(f * face, (f + 1) * face)
            theirs_l[rows, :] = jnp.zeros((face, cols), BF16)
            basis_n[rows, :] = jnp.zeros((face, nc1), BF16)
            xn[f] = jnp.zeros((cols, nc1), BF16)

    ld_cmap.wait()
    ld_l2map.wait()
    l2maps[grp] = jnp.broadcast_to(l2map[...], (8, nc2))
    ld_order.wait()
    order = order_s[...]
    ld_resid.wait()
    ld_basis.wait()
    basis = basis_s[...]

    def weigh(r, carry):
        rows = block(r, face)
        ids = lax.broadcasted_iota(jnp.int32, (face, n_if), 0) + r * face
        here = ids == order
        perm_t[rows, :] = jnp.where(here, F32(1.0), F32(0.0)).astype(BF16)
        dw = jnp.sum(jnp.where(here, all_weights, F32(0.0)), axis=1, keepdims=True)
        dofw[rows, :] = jnp.broadcast_to(dw, (face, LANES))
        weighted[rows, :] = (dw * resid[rows, :].astype(F32)).astype(BF16)
        return carry

    lax.fori_loop(0, 4, weigh, 0)
    coarse = dot(basis.astype(F32).T.astype(BF16), weighted[...])
    cres_t = coarse.T.astype(BF16)
    ld_l2basis.wait()
    l2basis_t = l2basis[...].T.astype(BF16)
    own_ids = lax.broadcasted_iota(jnp.int32, (ng2, nc1), 0)
    own_map = jnp.where(own_ids == cmap[...], F32(1.0), F32(0.0)).astype(BF16)
    own_rows = dot(l2basis_t, own_map).astype(BF16)
    t_src[...] = dot_t(cres_t, own_rows).astype(BF16).reshape(nsub, kc, nc2)
    c_src[:, 0:kc, :] = cres_t.reshape(nsub, kc, nc1)
    high = lax.shift_right_logical(cmap[...], 8)
    map_rows = jnp.concatenate(
        [high.astype(F32), (cmap[...] - high * 256).astype(F32), jnp.zeros((kc - 2, nc1), F32)], axis=0
    ).astype(BF16)
    c_src[:, kc : 2 * kc, :] = jnp.broadcast_to(map_rows[None], (nsub, kc, nc1))

    for load in loads[8:]:
        load.start()

    ld_linv.wait()
    wide = jnp.concatenate([dofw[...]] * (-(-cols // LANES)), axis=1)[:, :cols]
    scaled[...] = (wide * dot(linv[...], weighted[...])).astype(BF16)
    order_col = jnp.broadcast_to(order.astype(F32), (LANES, n_if)).T.astype(jnp.int32)

    def build_perm(b, carry):
        ids = lax.broadcasted_iota(jnp.int32, (n_if, LANES), 1) + b * LANES
        perm[:, block(b, LANES)] = jnp.where(ids == order_col, F32(1.0), F32(0.0)).astype(BF16)
        return carry

    lax.fori_loop(0, n_if // LANES, build_perm, 0)

    pl.semaphore_wait(barrier, nsub + ngrp - 2)

    def wait_bytes(ref, sem):
        pltpu.make_async_copy(ref, ref, sem).wait()

    def send_t(i, carry):
        t = peer_sub(i)
        pltpu.make_async_remote_copy(
            src_ref=t_src.at[t],
            dst_ref=t_recv.at[sub],
            send_sem=t_sem.at[0],
            recv_sem=t_sem.at[1],
            device_id={"sub": t},
            device_id_type=MESH,
        ).start()
        return carry

    def send_c(i, carry):
        t = peer_sub(i)
        pltpu.make_async_remote_copy(
            src_ref=c_src.at[t],
            dst_ref=c_recv.at[sub],
            send_sem=c_sem.at[0],
            recv_sem=c_sem.at[1],
            device_id={"sub": t},
            device_id_type=MESH,
        ).start()
        return carry

    def send_map3(i, carry):
        pltpu.make_async_remote_copy(
            src_ref=l2maps.at[grp],
            dst_ref=l2maps.at[grp],
            send_sem=map3_sem.at[0],
            recv_sem=map3_sem.at[1],
            device_id={"grp": peer_grp(i)},
            device_id_type=MESH,
        ).start()
        return carry

    lax.fori_loop(0, nsub - 1, send_t, 0)
    lax.fori_loop(0, nsub - 1, send_c, 0)
    lax.fori_loop(0, ngrp - 1, send_map3, 0)
    t_recv[sub] = t_src[sub]
    c_recv[sub] = c_src[sub]

    wait_bytes(t_recv.at[pl.ds(0, nsub - 1)], t_sem.at[1])
    term3[...] = jnp.sum(t_recv[...].astype(F32), axis=0)
    recv3[:, block(grp, nc2)] = term3[...]

    def send_z(i, carry):
        pltpu.make_async_remote_copy(
            src_ref=term3,
            dst_ref=recv3.at[:, block(grp, nc2)],
            send_sem=z_sem.at[0],
            recv_sem=z_sem.at[1],
            device_id={"grp": peer_grp(i)},
            device_id_type=MESH,
        ).start()
        return carry

    lax.fori_loop(0, ngrp - 1, send_z, 0)

    mine_l[...] = dot(perm[...], scaled[...]).astype(BF16)
    basis_f[...] = dot(perm[...], basis).astype(BF16)
    facing = (1, 0, 3, 2)

    def to_neighbour(f, src, dst, send_sem, recv_sem):
        axis, step = (("sub", -1), ("sub", 1), ("grp", -1), ("grp", 1))[f]
        size = nsub if axis == "sub" else ngrp
        return pltpu.make_async_remote_copy(
            src_ref=src,
            dst_ref=dst,
            send_sem=send_sem,
            recv_sem=recv_sem,
            device_id={axis: jnp.clip(lax.axis_index(axis) + step, 0, size - 1)},
            device_id_type=MESH,
        )

    for f in (2, 3, 0, 1):

        @pl.when(exists[f])
        def _(f=f):
            o = facing[f]
            rows, there = pl.ds(f * face, face), pl.ds(o * face, face)
            to_neighbour(f, mine_l.at[rows], theirs_l.at[there], lf_send.at[f], lf_recv.at[o]).start()
            to_neighbour(f, basis_f.at[rows], basis_n.at[there], bf_send.at[f], bf_recv.at[o]).start()

    wait_bytes(c_recv.at[pl.ds(0, nsub - 1)], c_sem.at[1])

    def build2(t, carry):
        recv2[:, block(t, nc1)] = c_recv[t, 0:kc, :]
        parts = c_recv[t, kc : 2 * kc, :].astype(F32)
        ids = lax.broadcasted_iota(jnp.int32, (ng2, nc1), 0)
        member = (parts[0:1] * 256.0 + parts[1:2]).astype(jnp.int32)
        onehot2[:, block(t, nc1)] = jnp.where(ids == member, F32(1.0), F32(0.0)).astype(BF16)
        return carry

    lax.fori_loop(0, nsub, build2, 0)
    ld_l2inv.wait()
    res2 = dot_t(recv2[...], onehot2[...])
    local2 = fold_terms(dot_t(two_terms(res2), l2inv[...].astype(BF16)))
    wait_bytes(l2maps.at[pl.ds(0, ngrp - 1)], map3_sem.at[1])

    def build3(t, carry):
        ids = lax.broadcasted_iota(jnp.int32, (ng3, nc2), 0)
        onehot3[:, block(t, nc2)] = jnp.where(ids == l2maps[t][0:1], F32(1.0), F32(0.0)).astype(BF16)
        return carry

    lax.fori_loop(0, ngrp, build3, 0)
    ld_l3inv.wait()
    own3 = onehot3[:, block(grp, nc2)].astype(F32).T.astype(BF16)
    l3rows = dot(own3, l3inv[...].astype(BF16)).astype(BF16)
    q3[...] = dot(l3rows, onehot3[...]).astype(BF16)

    wait_bytes(recv3.at[:, pl.ds(0, (ngrp - 1) * nc2)], z_sem.at[1])
    picked = two_terms(fold_terms(dot_t(two_terms(recv3[...]), q3[...])))
    sol2 = (local2 + fold_terms(dot(picked, l2basis_t))).astype(BF16)
    wide2 = min(1024, nsub * nc1)

    def spread(j, carry):
        back[:, block(j, wide2)] = dot(sol2, onehot2[:, block(j, wide2)]).astype(BF16)
        return carry

    lax.fori_loop(0, nsub * nc1 // wide2, spread, 0)

    def send_back(i, carry):
        t = peer_sub(i)
        pltpu.make_async_remote_copy(
            src_ref=back.at[:, block(t, nc1)],
            dst_ref=xcoef.at[block(sub, kc), :],
            send_sem=back_sem.at[0],
            recv_sem=back_sem.at[1],
            device_id={"sub": t},
            device_id_type=MESH,
        ).start()
        return carry

    lax.fori_loop(0, nsub - 1, send_back, 0)
    xcoef[block(sub, kc), :] = back[:, block(sub, nc1)]

    ld_schur.wait()
    wide_p = n_if // 2

    def permute_schur(j, carry):
        schur_p[:, block(j, wide_p)] = dot(schur[...], perm_t[:, block(j, wide_p)]).astype(BF16)
        return carry

    lax.fori_loop(0, n_if // wide_p, permute_schur, 0)

    wait_bytes(xcoef.at[pl.ds(0, (nsub - 1) * kc), :], back_sem.at[1])
    for h in range(2):
        part = pl.ds(h * half, half)
        for f in (2, 3, 0, 1):

            @pl.when(exists[f])
            def _(f=f, h=h, part=part):
                o = facing[f]
                to_neighbour(f, xcoef.at[part], xn.at[o, part], xf_send.at[f, h], xf_recv.at[o, h]).start()

    coarse_part = dot_t(basis_f[...], xcoef[...])
    for f in range(4):
        rows = slice(f * face, (f + 1) * face)
        mine[rows, :] = (mine_l[rows, :].astype(F32) + weights[f][:, 0:1] * coarse_part[rows]).astype(BF16)

    def received(f, h):
        @pl.when(exists[f])
        def _():
            wait_bytes(xn.at[f, pl.ds(h * half, half)], xf_recv.at[f, h])
            if h == 0:
                wait_bytes(theirs_l.at[pl.ds(f * face, face)], lf_recv.at[f])
                wait_bytes(basis_n.at[pl.ds(f * face, face)], bf_recv.at[f])

        rows, here = slice(f * face, (f + 1) * face), slice(h * half, (h + 1) * half)
        part = dot_t(basis_n[rows, :], xn[f, here, :])
        theirs = (theirs_l[rows, here].astype(F32) + their_weights[f][:, 0:1] * part).astype(BF16)
        return (mine[rows, here].astype(F32) + theirs.astype(F32)).astype(BF16)

    for h in range(2):
        here = slice(h * half, (h + 1) * half)
        lower = jnp.concatenate([received(0, h), received(1, h)], axis=0)
        sol_acc[:, here] = dot(perm_t[:, 0 : 2 * face], lower).astype(BF16)
        img_acc[:, here] = dot(schur_p[:, 0 : 2 * face], lower)

    stores = []
    for h in range(2):
        here = slice(h * half, (h + 1) * half)
        upper = jnp.concatenate([received(2, h), received(3, h)], axis=0)
        sol[:, here] = (sol_acc[:, here].astype(F32) + dot(perm_t[:, 2 * face :], upper)).astype(BF16)
        img[:, here] = (img_acc[:, here] + dot(schur_p[:, 2 * face :], upper)).astype(BF16)
        for i, (src, dst) in enumerate([(sol, sol_h), (img, img_h)]):
            there = pl.ds(h * half, half)
            done = pltpu.make_async_copy(src.at[:, there], dst.at[0, 0, :, there], out_sem.at[i, h])
            done.start()
            stores.append(done)

    wait_bytes(t_src.at[pl.ds(0, nsub - 1)], t_sem.at[0])
    wait_bytes(c_src.at[pl.ds(0, nsub - 1)], c_sem.at[0])
    wait_bytes(l2maps.at[pl.ds(0, ngrp - 1)], map3_sem.at[0])
    wait_bytes(recv3.at[:, pl.ds(0, (ngrp - 1) * nc2)], z_sem.at[0])
    wait_bytes(back.at[:, pl.ds(0, (nsub - 1) * nc1)], back_sem.at[0])
    for f in range(4):

        @pl.when(exists[f])
        def _(f=f):
            rows = pl.ds(f * face, face)
            wait_bytes(mine_l.at[rows], lf_send.at[f])
            wait_bytes(basis_f.at[rows], bf_send.at[f])
            for h in range(2):
                wait_bytes(xcoef.at[pl.ds(h * half, half)], xf_send.at[f, h])

    for done in stores:
        done.wait()


def store(parts, sol, img, sol_h, img_h, sol_v, img_v, in_sem, out_sem):
    size = sol_v.shape[0] // parts
    moves = []
    for i in range(parts):
        rows = pl.ds(i * size, size)
        for j, (src, via, dst) in enumerate([(sol, sol_v, sol_h), (img, img_v, img_h)]):
            load = pltpu.make_async_copy(src.at[0, 0, rows], via.at[rows], in_sem.at[j, i])
            moves.append((load, pltpu.make_async_copy(via.at[rows], dst.at[0, 0, rows], out_sem.at[j, i])))
            load.start()
    for load, save in moves:
        load.wait()
        save.start()
    for load, save in moves:
        save.wait()


def shards(nsub, ngrp, *args):
    resid, order, stiff, schur, linv, basis, cmap, l2inv, l2basis, l2map, l3inv = args
    n_if, cols = resid.shape[2:]
    nc1 = basis.shape[3]
    ng2, nc2 = l2basis.shape[1:]
    ng3 = l3inv.shape[0]
    kc = cols // nsub
    vmem = pltpu.VMEM
    dma = pltpu.SemaphoreType.DMA
    scratch = [
        vmem((n_if, cols), BF16),
        vmem((1, n_if), jnp.int32),
        vmem((n_if, nc1), BF16),
        vmem((1, nc1), jnp.int32),
        vmem((1, nc2), jnp.int32),
        pltpu.SMEM((ngrp, nsub), F32),
        vmem((n_if, n_if), BF16),
        vmem((n_if, n_if), BF16),
        vmem((ng2, ng2), F32),
        vmem((ng2, nc2), F32),
        vmem((ng3, ng3), F32),
        vmem((ngrp, 8, nc2), jnp.int32),
        vmem((n_if, n_if), BF16),
        vmem((n_if, n_if), BF16),
        vmem((n_if, LANES), F32),
        vmem((n_if, cols), BF16),
        vmem((nsub, kc, nc2), BF16),
        vmem((nsub, kc, nc2), BF16),
        vmem((nsub, 2 * kc, nc1), BF16),
        vmem((nsub, 2 * kc, nc1), BF16),
        vmem((kc, nsub * nc1), BF16),
        vmem((ng2, nsub * nc1), BF16),
        vmem((ng3, ngrp * nc2), BF16),
        vmem((nc2, ngrp * nc2), BF16),
        vmem((kc, ngrp * nc2), F32),
        vmem((kc, nc2), F32),
        vmem((kc, nsub * nc1), BF16),
        vmem((cols, nc1), BF16),
        vmem((4, cols, nc1), BF16),
        vmem((n_if, cols), BF16),
        vmem((n_if, cols), BF16),
        vmem((n_if, cols), BF16),
        vmem((n_if, nc1), BF16),
        vmem((n_if, nc1), BF16),
        vmem((n_if, n_if), BF16),
        vmem((n_if, cols), BF16),
        vmem((n_if, cols), BF16),
        vmem((n_if, cols), F32),
        vmem((n_if, cols), BF16),
        vmem((n_if, cols), BF16),
        dma((11,)),
        dma((2, 2)),
        dma((2,)),
        dma((2,)),
        dma((2,)),
        dma((2,)),
        dma((2,)),
        dma((4,)),
        dma((4,)),
        dma((4,)),
        dma((4,)),
        dma((4, 2)),
        dma((4, 2)),
    ]
    flops = 2 * n_if * cols * n_if * 4 + 2 * n_if**3
    out = jax.ShapeDtypeStruct((1, 1, n_if, cols), BF16)
    any_ = pl.BlockSpec(memory_space=pl.ANY)
    done = pl.pallas_call(
        functools.partial(kernel, nsub, ngrp),
        out_shape=(out, out),
        in_specs=[any_] * 11,
        out_specs=(any_, any_),
        scratch_shapes=scratch,
        compiler_params=pltpu.CompilerParams(
            collective_id=0, has_side_effects=True, vmem_limit_bytes=60 * 1024 * 1024
        ),
        cost_estimate=pl.CostEstimate(flops=flops, bytes_accessed=11 << 20, transcendentals=0),
        name="bddc_apply",
    )(*args)
    return pl.pallas_call(
        functools.partial(store, 4),
        out_shape=(out, out),
        in_specs=[any_, any_],
        out_specs=(any_, any_),
        scratch_shapes=[vmem((n_if, cols), BF16), vmem((n_if, cols), BF16), dma((2, 4)), dma((2, 4))],
        compiler_params=pltpu.CompilerParams(vmem_limit_bytes=60 * 1024 * 1024),
        name="store",
    )(*done)


def solution(mesh):
    placed = (
        P("grp", "sub", None, None),
        P("grp", "sub", None),
        P(),
        P("grp", "sub", None, None),
        P("grp", "sub", None, None),
        P("grp", "sub", None, None),
        P("grp", "sub", None),
        P("grp", None, None),
        P("grp", None, None),
        P("grp", None),
        P(),
    )
    return jax.shard_map(
        functools.partial(shards, mesh.shape["sub"], mesh.shape["grp"]),
        mesh=mesh,
        in_specs=placed,
        out_specs=(P("grp", "sub", None, None), P("grp", "sub", None, None)),
        check_vma=False,
    )
```

time: 114 us -> 41 us (0.36)
  Pallas kernels: 105 us -> 40.3 us
  local copies, waits for them, and re-layouts: 7.78 us -> 0 us
    pallas_call x1, Pallas kernels: 64.6 us -> 2.39 us  [shards(): pl.pallas_call(functools.partial(store, 4), out_shape=(out, out), in_spec...]
    unnamed x18 -> x0, local copies, waits for them, and re-layouts: 7.78 us -> none
    pallas_call x1, Pallas kernels: 40.3 us -> 37.9 us  [shards(): pl.pallas_call(functools.partial(kernel, nsub, ngrp), out_shape=(out, out...]
where the time goes in v3:
time: 41 us; the launch traced here: 40.9 us
  Pallas kernels  40.3 us (98%)
  between operations  0.64 us (2%)
    pallas_call x1, Pallas kernels, shards(): pl.pallas_call(functools.partial(kernel, nsub, ngrp), out_shape=(out, out...  37.9 us
    pallas_call x1, Pallas kernels, shards(): pl.pallas_call(functools.partial(store, 4), out_shape=(out, out), in_spec...  2.39 us

profile of v3, /device:TPU:1, one launch (start us, length us, event | category | flops | bytes accessed | tf_op | source)
XLA Modules:
  0.0 40.9 jit_solution(7103330930907541271)
XLA Ops:
  0.6 37.9 %bddc_apply.1 = (bf16[1,1,1024,512]{3,2,1,0:T(8,128)(2,1)}, bf16[1,1,1024,512]{3,2,1,0:T(8,128)(2,1)}) custom-call(bf16[1,1,1024,512]{3,2,1,0:T(8,128)(2,1)} %resid_h.1, s32[1,1,1024]{2,1,0:T(1,128)} %order_h.1, f32[8,32]{1,0:T(8,128)} %stiff_h.1, bf16[1,1,1024,1024]{3,2,1,0:T(8,128)(2,1)} %schur_h.1, bf16[1,1,1024,1024]{3,2,1,0:T(8,128)(2,1)} %linv_h.1, ...), custom_call_target="tpu_custom_call" | custom-call | flops 6442450944 | bytes 11534336 | tf_op jit(solution)/shard_map/bddc_apply/pallas_call | solution.py:541
  38.5 2.4 %store.1 = (bf16[1,1,1024,512]{3,2,1,0:T(8,128)(2,1)}, bf16[1,1,1024,512]{3,2,1,0:T(8,128)(2,1)}) custom-call(bf16[1,1,1024,512]{3,2,1,0:T(8,128)(2,1)} %get-tuple-element.4.sol, bf16[1,1,1024,512]{3,2,1,0:T(8,128)(2,1)} %get-tuple-element.5.img), custom_call_target="tpu_custom_call" | custom-call | tf_op jit(solution)/shard_map/store/pallas_call | solution.py:553

commit v4 on v3

--- a/solution.py
+++ b/solution.py
@@ -34,6 +34,11 @@
 
 def block(index, size):
     return pl.ds(pl.multiple_of(index * size, size), size)
+
+
+def plane(nsub):
+    nx = 4 if nsub % 8 == 0 else 2
+    return nx, nsub // (2 * nx)
 
 
 def far_first(r):
@@ -83,6 +88,7 @@
     recv3,
     term3,
     back,
+    xtwo,
     xcoef,
     xn,
     scaled,
@@ -91,7 +97,8 @@
     basis_f,
     basis_n,
     schur_p,
-    mine,
+    base,
+    pair,
     sol_acc,
     img_acc,
     sol,
@@ -109,6 +116,8 @@
     bf_recv,
     xf_send,
     xf_recv,
+    xz_send,
+    xz_recv,
 ):
     grp = lax.axis_index("grp")
     sub = lax.axis_index("sub")
@@ -142,8 +151,7 @@
         load.start()
     ld_order, ld_stiff, ld_cmap, ld_l2map, ld_resid, ld_basis, ld_l2basis, ld_linv, ld_l2inv, ld_l3inv, ld_schur = loads
 
-    nx = 4 if nsub % 8 == 0 else 2
-    ny = nsub // (2 * nx)
+    nx, ny = plane(nsub)
     at_y, at_x, at_c = lax.div(sub, 2 * nx), lax.rem(lax.div(sub, 2), nx), lax.rem(sub, 2)
 
     def peer_sub(i):
@@ -181,6 +189,8 @@
         their_weights.append((nbr / (nbr + num))[0:1])
     all_weights = jnp.concatenate(weights, axis=1)
 
+    onehot2[:, 0:nc1] = jnp.zeros((ng2, nc1), BF16)
+    onehot2[:, (nsub + 1) * nc1 :] = jnp.zeros((ng2, nc1), BF16)
     for f in range(4):
 
         @pl.when(jnp.logical_not(exists[f]))
@@ -228,18 +238,6 @@
     for load in loads[8:]:
         load.start()
 
-    ld_linv.wait()
-    wide = jnp.concatenate([dofw[...]] * (-(-cols // LANES)), axis=1)[:, :cols]
-    scaled[...] = (wide * dot(linv[...], weighted[...])).astype(BF16)
-    order_col = jnp.broadcast_to(order.astype(F32), (LANES, n_if)).T.astype(jnp.int32)
-
-    def build_perm(b, carry):
-        ids = lax.broadcasted_iota(jnp.int32, (n_if, LANES), 1) + b * LANES
-        perm[:, block(b, LANES)] = jnp.where(ids == order_col, F32(1.0), F32(0.0)).astype(BF16)
-        return carry
-
-    lax.fori_loop(0, n_if // LANES, build_perm, 0)
-
     pl.semaphore_wait(barrier, nsub + ngrp - 2)
 
     def wait_bytes(ref, sem):
@@ -281,10 +279,22 @@
         return carry
 
     lax.fori_loop(0, nsub - 1, send_t, 0)
+    lax.fori_loop(0, ngrp - 1, send_map3, 0)
     lax.fori_loop(0, nsub - 1, send_c, 0)
-    lax.fori_loop(0, ngrp - 1, send_map3, 0)
     t_recv[sub] = t_src[sub]
     c_recv[sub] = c_src[sub]
+
+    ld_linv.wait()
+    wide = jnp.concatenate([dofw[...]] * (-(-cols // LANES)), axis=1)[:, :cols]
+    scaled[...] = (wide * dot(linv[...], weighted[...])).astype(BF16)
+    order_col = jnp.broadcast_to(order.astype(F32), (LANES, n_if)).T.astype(jnp.int32)
+
+    def build_perm(b, carry):
+        ids = lax.broadcasted_iota(jnp.int32, (n_if, LANES), 1) + b * LANES
+        perm[:, block(b, LANES)] = jnp.where(ids == order_col, F32(1.0), F32(0.0)).astype(BF16)
+        return carry
+
+    lax.fori_loop(0, n_if // LANES, build_perm, 0)
 
     wait_bytes(t_recv.at[pl.ds(0, nsub - 1)], t_sem.at[1])
     term3[...] = jnp.sum(t_recv[...].astype(F32), axis=0)
@@ -328,6 +338,19 @@
             to_neighbour(f, mine_l.at[rows], theirs_l.at[there], lf_send.at[f], lf_recv.at[o]).start()
             to_neighbour(f, basis_f.at[rows], basis_n.at[there], bf_send.at[f], bf_recv.at[o]).start()
 
+    wait_bytes(l2maps.at[pl.ds(0, ngrp - 1)], map3_sem.at[1])
+
+    def build3(t, carry):
+        ids = lax.broadcasted_iota(jnp.int32, (ng3, nc2), 0)
+        onehot3[:, block(t, nc2)] = jnp.where(ids == l2maps[t][0:1], F32(1.0), F32(0.0)).astype(BF16)
+        return carry
+
+    lax.fori_loop(0, ngrp, build3, 0)
+    ld_l3inv.wait()
+    own3 = onehot3[:, block(grp, nc2)].astype(F32).T.astype(BF16)
+    l3rows = dot(own3, l3inv[...].astype(BF16)).astype(BF16)
+    q3[...] = dot(l3rows, onehot3[...]).astype(BF16)
+
     wait_bytes(c_recv.at[pl.ds(0, nsub - 1)], c_sem.at[1])
 
     def build2(t, carry):
@@ -335,112 +358,135 @@
         parts = c_recv[t, kc : 2 * kc, :].astype(F32)
         ids = lax.broadcasted_iota(jnp.int32, (ng2, nc1), 0)
         member = (parts[0:1] * 256.0 + parts[1:2]).astype(jnp.int32)
-        onehot2[:, block(t, nc1)] = jnp.where(ids == member, F32(1.0), F32(0.0)).astype(BF16)
+        onehot2[:, block(t + 1, nc1)] = jnp.where(ids == member, F32(1.0), F32(0.0)).astype(BF16)
         return carry
 
     lax.fori_loop(0, nsub, build2, 0)
     ld_l2inv.wait()
-    res2 = dot_t(recv2[...], onehot2[...])
+    res2 = dot_t(recv2[...], onehot2[:, nc1 : (nsub + 1) * nc1])
     local2 = fold_terms(dot_t(two_terms(res2), l2inv[...].astype(BF16)))
-    wait_bytes(l2maps.at[pl.ds(0, ngrp - 1)], map3_sem.at[1])
-
-    def build3(t, carry):
-        ids = lax.broadcasted_iota(jnp.int32, (ng3, nc2), 0)
-        onehot3[:, block(t, nc2)] = jnp.where(ids == l2maps[t][0:1], F32(1.0), F32(0.0)).astype(BF16)
-        return carry
-
-    lax.fori_loop(0, ngrp, build3, 0)
-    ld_l3inv.wait()
-    own3 = onehot3[:, block(grp, nc2)].astype(F32).T.astype(BF16)
-    l3rows = dot(own3, l3inv[...].astype(BF16)).astype(BF16)
-    q3[...] = dot(l3rows, onehot3[...]).astype(BF16)
 
     wait_bytes(recv3.at[:, pl.ds(0, (ngrp - 1) * nc2)], z_sem.at[1])
     picked = two_terms(fold_terms(dot_t(two_terms(recv3[...]), q3[...])))
     sol2 = (local2 + fold_terms(dot(picked, l2basis_t))).astype(BF16)
-    wide2 = min(1024, nsub * nc1)
-
-    def spread(j, carry):
-        back[:, block(j, wide2)] = dot(sol2, onehot2[:, block(j, wide2)]).astype(BF16)
-        return carry
-
-    lax.fori_loop(0, nsub * nc1 // wide2, spread, 0)
-
-    def send_back(i, carry):
+    row = 2 * nx
+    odd = lax.rem(sub, 2)
+
+    def two(t):
+        return pl.ds(pl.multiple_of((lax.rem(t, row) + lax.rem(t, 2)) * nc1, nc1), 2 * nc1)
+
+    def spread(r, carry):
+        far = ny - 1 - r
+        y = lax.rem(at_y + far_first(far), ny)
+        here = pl.ds(pl.multiple_of(y * row * nc1, nc1), (row + 2) * nc1)
+        back[y] = dot(sol2, onehot2[:, here]).astype(BF16)
+
+        def send_back(i, carry):
+            j = row - 1 - i
+            x = lax.rem(at_x + far_first(lax.div(j, 2)), nx)
+            t = (y * nx + x) * 2 + lax.rem(at_c + lax.rem(j, 2), 2)
+
+            @pl.when(t != sub)
+            def _():
+                pltpu.make_async_remote_copy(
+                    src_ref=back.at[y, :, two(t)],
+                    dst_ref=xtwo.at[block(sub, kc), :],
+                    send_sem=back_sem.at[0],
+                    recv_sem=back_sem.at[1],
+                    device_id={"sub": t},
+                    device_id_type=MESH,
+                ).start()
+
+            return carry
+
+        return lax.fori_loop(0, row, send_back, carry)
+
+    lax.fori_loop(0, ny, spread, 0)
+    xtwo[block(sub, kc), :] = back[at_y, :, two(sub)]
+
+    def send_across(i, carry):
         t = peer_sub(i)
-        pltpu.make_async_remote_copy(
-            src_ref=back.at[:, block(t, nc1)],
-            dst_ref=xcoef.at[block(sub, kc), :],
-            send_sem=back_sem.at[0],
-            recv_sem=back_sem.at[1],
-            device_id={"sub": t},
-            device_id_type=MESH,
-        ).start()
-        return carry
-
-    lax.fori_loop(0, nsub - 1, send_back, 0)
-    xcoef[block(sub, kc), :] = back[:, block(sub, nc1)]
+        for f, step in ((2, -1), (3, 1)):
+
+            @pl.when(exists[f])
+            def _(f=f, step=step):
+                pltpu.make_async_remote_copy(
+                    src_ref=back.at[lax.div(t, row), :, block(lax.rem(t, row) + 1, nc1)],
+                    dst_ref=xn.at[facing[f], block(sub, kc), :],
+                    send_sem=xz_send.at[f - 2],
+                    recv_sem=xz_recv.at[facing[f] - 2],
+                    device_id={"sub": t, "grp": jnp.clip(grp + step, 0, ngrp - 1)},
+                    device_id_type=MESH,
+                ).start()
+
+        return carry
+
+    lax.fori_loop(0, nsub, send_across, 0)
 
     ld_schur.wait()
     wide_p = n_if // 2
-
-    def permute_schur(j, carry):
-        schur_p[:, block(j, wide_p)] = dot(schur[...], perm_t[:, block(j, wide_p)]).astype(BF16)
-        return carry
-
-    lax.fori_loop(0, n_if // wide_p, permute_schur, 0)
-
-    wait_bytes(xcoef.at[pl.ds(0, (nsub - 1) * kc), :], back_sem.at[1])
-    for h in range(2):
-        part = pl.ds(h * half, half)
-        for f in (2, 3, 0, 1):
-
-            @pl.when(exists[f])
-            def _(f=f, h=h, part=part):
-                o = facing[f]
-                to_neighbour(f, xcoef.at[part], xn.at[o, part], xf_send.at[f, h], xf_recv.at[o, h]).start()
-
-    coarse_part = dot_t(basis_f[...], xcoef[...])
+    schur_p[:, 0:wide_p] = dot(schur[...], perm_t[:, 0:wide_p]).astype(BF16)
+
+    wait_bytes(xtwo.at[pl.ds(0, (nsub - 1) * kc), :], back_sem.at[1])
+    xcoef[...] = xtwo[:, block(1 - odd, nc1)]
+    xn[odd] = xtwo[:, block(odd, nc1)]
+    pltpu.make_async_remote_copy(
+        src_ref=xcoef,
+        dst_ref=xn.at[odd],
+        send_sem=xf_send.at[0],
+        recv_sem=xf_recv.at[0],
+        device_id={"sub": sub + 1 - 2 * odd},
+        device_id_type=MESH,
+    ).start()
+
+    schur_p[:, wide_p:] = dot(schur[...], perm_t[:, wide_p:]).astype(BF16)
+
     for f in range(4):
+
+        @pl.when(exists[f])
+        def _(f=f):
+            wait_bytes(theirs_l.at[pl.ds(f * face, face)], lf_recv.at[f])
+            wait_bytes(basis_n.at[pl.ds(f * face, face)], bf_recv.at[f])
+
         rows = slice(f * face, (f + 1) * face)
-        mine[rows, :] = (mine_l[rows, :].astype(F32) + weights[f][:, 0:1] * coarse_part[rows]).astype(BF16)
-
-    def received(f, h):
+        base[rows, :] = mine_l[rows, :].astype(F32) + theirs_l[rows, :].astype(F32)
+        pair[rows, 0:nc1] = (weights[f][:, 0:1] * basis_f[rows, :].astype(F32)).astype(BF16)
+        pair[rows, nc1:] = (their_weights[f][:, 0:1] * basis_n[rows, :].astype(F32)).astype(BF16)
+
+    def summed(f, here):
+        rows = slice(f * face, (f + 1) * face)
+        both = jnp.concatenate([xcoef[here, :], xn[f, here, :]], axis=1)
+        return (base[rows, here] + dot_t(pair[rows, :], both)).astype(BF16)
+
+    for f in (2, 3):
+
         @pl.when(exists[f])
-        def _():
-            wait_bytes(xn.at[f, pl.ds(h * half, half)], xf_recv.at[f, h])
-            if h == 0:
-                wait_bytes(theirs_l.at[pl.ds(f * face, face)], lf_recv.at[f])
-                wait_bytes(basis_n.at[pl.ds(f * face, face)], bf_recv.at[f])
-
-        rows, here = slice(f * face, (f + 1) * face), slice(h * half, (h + 1) * half)
-        part = dot_t(basis_n[rows, :], xn[f, here, :])
-        theirs = (theirs_l[rows, here].astype(F32) + their_weights[f][:, 0:1] * part).astype(BF16)
-        return (mine[rows, here].astype(F32) + theirs.astype(F32)).astype(BF16)
-
-    for h in range(2):
-        here = slice(h * half, (h + 1) * half)
-        lower = jnp.concatenate([received(0, h), received(1, h)], axis=0)
-        sol_acc[:, here] = dot(perm_t[:, 0 : 2 * face], lower).astype(BF16)
-        img_acc[:, here] = dot(schur_p[:, 0 : 2 * face], lower)
-
+        def _(f=f):
+            wait_bytes(xn.at[f], xz_recv.at[f - 2])
+
+    upper = jnp.concatenate([summed(2, slice(0, cols)), summed(3, slice(0, cols))], axis=0)
+    sol_acc[...] = dot(perm_t[:, 2 * face :], upper).astype(BF16)
+    img_acc[...] = dot(schur_p[:, 2 * face :], upper)
+
+    wait_bytes(xn.at[1 - odd], xf_recv.at[0])
     stores = []
     for h in range(2):
         here = slice(h * half, (h + 1) * half)
-        upper = jnp.concatenate([received(2, h), received(3, h)], axis=0)
-        sol[:, here] = (sol_acc[:, here].astype(F32) + dot(perm_t[:, 2 * face :], upper)).astype(BF16)
-        img[:, here] = (img_acc[:, here] + dot(schur_p[:, 2 * face :], upper)).astype(BF16)
-        for i, (src, dst) in enumerate([(sol, sol_h), (img, img_h)]):
-            there = pl.ds(h * half, half)
-            done = pltpu.make_async_copy(src.at[:, there], dst.at[0, 0, :, there], out_sem.at[i, h])
-            done.start()
-            stores.append(done)
+        lower = jnp.concatenate([summed(0, here), summed(1, here)], axis=0)
+        there = pl.ds(h * half, half)
+        sol[:, here] = (sol_acc[:, here].astype(F32) + dot(perm_t[:, 0 : 2 * face], lower)).astype(BF16)
+        stores.append(pltpu.make_async_copy(sol.at[:, there], sol_h.at[0, 0, :, there], out_sem.at[0, h]))
+        stores[-1].start()
+        img[:, here] = (img_acc[:, here] + dot(schur_p[:, 0 : 2 * face], lower)).astype(BF16)
+        stores.append(pltpu.make_async_copy(img.at[:, there], img_h.at[0, 0, :, there], out_sem.at[1, h]))
+        stores[-1].start()
 
     wait_bytes(t_src.at[pl.ds(0, nsub - 1)], t_sem.at[0])
     wait_bytes(c_src.at[pl.ds(0, nsub - 1)], c_sem.at[0])
     wait_bytes(l2maps.at[pl.ds(0, ngrp - 1)], map3_sem.at[0])
     wait_bytes(recv3.at[:, pl.ds(0, (ngrp - 1) * nc2)], z_sem.at[0])
-    wait_bytes(back.at[:, pl.ds(0, (nsub - 1) * nc1)], back_sem.at[0])
+    wait_bytes(xtwo.at[pl.ds(0, (nsub - 1) * kc), :], back_sem.at[0])
+    wait_bytes(xcoef, xf_send.at[0])
     for f in range(4):
 
         @pl.when(exists[f])
@@ -448,8 +494,8 @@
             rows = pl.ds(f * face, face)
             wait_bytes(mine_l.at[rows], lf_send.at[f])
             wait_bytes(basis_f.at[rows], bf_send.at[f])
-            for h in range(2):
-                wait_bytes(xcoef.at[pl.ds(h * half, half)], xf_send.at[f, h])
+            if f >= 2:
+                wait_bytes(xn.at[f], xz_send.at[f - 2])
 
     for done in stores:
         done.wait()
@@ -478,6 +524,7 @@
     ng2, nc2 = l2basis.shape[1:]
     ng3 = l3inv.shape[0]
     kc = cols // nsub
+    nx, ny = plane(nsub)
     vmem = pltpu.VMEM
     dma = pltpu.SemaphoreType.DMA
     scratch = [
@@ -502,12 +549,13 @@
         vmem((nsub, 2 * kc, nc1), BF16),
         vmem((nsub, 2 * kc, nc1), BF16),
         vmem((kc, nsub * nc1), BF16),
-        vmem((ng2, nsub * nc1), BF16),
+        vmem((ng2, (nsub + 2) * nc1), BF16),
         vmem((ng3, ngrp * nc2), BF16),
         vmem((nc2, ngrp * nc2), BF16),
         vmem((kc, ngrp * nc2), F32),
         vmem((kc, nc2), F32),
-        vmem((kc, nsub * nc1), BF16),
+        vmem((ny, kc, (2 * nx + 2) * nc1), BF16),
+        vmem((cols, 2 * nc1), BF16),
         vmem((cols, nc1), BF16),
         vmem((4, cols, nc1), BF16),
         vmem((n_if, cols), BF16),
@@ -516,7 +564,8 @@
         vmem((n_if, nc1), BF16),
         vmem((n_if, nc1), BF16),
         vmem((n_if, n_if), BF16),
-        vmem((n_if, cols), BF16),
+        vmem((n_if, cols), F32),
+        vmem((n_if, 2 * nc1), BF16),
         vmem((n_if, cols), BF16),
         vmem((n_if, cols), F32),
         vmem((n_if, cols), BF16),
@@ -532,8 +581,10 @@
         dma((4,)),
         dma((4,)),
         dma((4,)),
-        dma((4, 2)),
-        dma((4, 2)),
+        dma((1,)),
+        dma((1,)),
+        dma((2,)),
+        dma((2,)),
     ]
     flops = 2 * n_if * cols * n_if * 4 + 2 * n_if**3
     out = jax.ShapeDtypeStruct((1, 1, n_if, cols), BF16)

time: 41 us -> 39.9 us (0.973)
  Pallas kernels: 40.3 us -> 39.2 us
    pallas_call x1, Pallas kernels: 37.9 us -> 36.8 us  [shards(): pl.pallas_call(functools.partial(kernel, nsub, ngrp), out_shape=(out, out...]
where the time goes in v4:
time: 39.9 us; the launch traced here: 39.8 us
  Pallas kernels  39.2 us (98%)
  between operations  0.64 us (2%)
    pallas_call x1, Pallas kernels, shards(): pl.pallas_call(functools.partial(kernel, nsub, ngrp), out_shape=(out, out...  36.8 us
    pallas_call x1, Pallas kernels, shards(): pl.pallas_call(functools.partial(store, 4), out_shape=(out, out), in_spec...  2.39 us

profile of v4, /device:TPU:1, one launch (start us, length us, event | category | flops | bytes accessed | tf_op | source)
XLA Modules:
  0.0 39.8 jit_solution(19223452970710305)
XLA Ops:
  0.6 36.8 %bddc_apply.1 = (bf16[1,1,1024,512]{3,2,1,0:T(8,128)(2,1)}, bf16[1,1,1024,512]{3,2,1,0:T(8,128)(2,1)}) custom-call(bf16[1,1,1024,512]{3,2,1,0:T(8,128)(2,1)} %resid_h.1, s32[1,1,1024]{2,1,0:T(1,128)} %order_h.1, f32[8,32]{1,0:T(8,128)} %stiff_h.1, bf16[1,1,1024,1024]{3,2,1,0:T(8,128)(2,1)} %schur_h.1, bf16[1,1,1024,1024]{3,2,1,0:T(8,128)(2,1)} %linv_h.1, ...), custom_call_target="tpu_custom_call" | custom-call | flops 6442450944 | bytes 11534336 | tf_op jit(solution)/shard_map/bddc_apply/pallas_call | solution.py:592
  37.4 2.4 %store.1 = (bf16[1,1,1024,512]{3,2,1,0:T(8,128)(2,1)}, bf16[1,1,1024,512]{3,2,1,0:T(8,128)(2,1)}) custom-call(bf16[1,1,1024,512]{3,2,1,0:T(8,128)(2,1)} %get-tuple-element.4.sol, bf16[1,1,1024,512]{3,2,1,0:T(8,128)(2,1)} %get-tuple-element.5.img), custom_call_target="tpu_custom_call" | custom-call | tf_op jit(solution)/shard_map/store/pallas_call | solution.py:604

commit v5 on v4

--- a/solution.py
+++ b/solution.py
@@ -137,9 +137,9 @@
                 (stiff_h, stiff),
                 (cmap_h.at[0], cmap),
                 (l2map_h, l2map),
-                (resid_h.at[0, 0], resid),
                 (basis_h.at[0, 0], basis_s),
                 (l2basis_h.at[0], l2basis),
+                (resid_h.at[0, 0], resid),
                 (linv_h.at[0, 0], linv),
                 (l2inv_h.at[0], l2inv),
                 (l3inv_h, l3inv),
@@ -149,7 +149,7 @@
     ]
     for load in loads[:8]:
         load.start()
-    ld_order, ld_stiff, ld_cmap, ld_l2map, ld_resid, ld_basis, ld_l2basis, ld_linv, ld_l2inv, ld_l3inv, ld_schur = loads
+    ld_order, ld_stiff, ld_cmap, ld_l2map, ld_basis, ld_l2basis, ld_resid, ld_linv, ld_l2inv, ld_l3inv, ld_schur = loads
 
     nx, ny = plane(nsub)
     at_y, at_x, at_c = lax.div(sub, 2 * nx), lax.rem(lax.div(sub, 2), nx), lax.rem(sub, 2)
@@ -205,9 +205,6 @@
     l2maps[grp] = jnp.broadcast_to(l2map[...], (8, nc2))
     ld_order.wait()
     order = order_s[...]
-    ld_resid.wait()
-    ld_basis.wait()
-    basis = basis_s[...]
 
     def weigh(r, carry):
         rows = block(r, face)
@@ -216,27 +213,31 @@
         perm_t[rows, :] = jnp.where(here, F32(1.0), F32(0.0)).astype(BF16)
         dw = jnp.sum(jnp.where(here, all_weights, F32(0.0)), axis=1, keepdims=True)
         dofw[rows, :] = jnp.broadcast_to(dw, (face, LANES))
-        weighted[rows, :] = (dw * resid[rows, :].astype(F32)).astype(BF16)
         return carry
 
     lax.fori_loop(0, 4, weigh, 0)
-    coarse = dot(basis.astype(F32).T.astype(BF16), weighted[...])
-    cres_t = coarse.T.astype(BF16)
+    ld_basis.wait()
+    basis = basis_s[...]
+    basis_t = basis.astype(F32).T.astype(BF16)
     ld_l2basis.wait()
     l2basis_t = l2basis[...].T.astype(BF16)
     own_ids = lax.broadcasted_iota(jnp.int32, (ng2, nc1), 0)
     own_map = jnp.where(own_ids == cmap[...], F32(1.0), F32(0.0)).astype(BF16)
     own_rows = dot(l2basis_t, own_map).astype(BF16)
-    t_src[...] = dot_t(cres_t, own_rows).astype(BF16).reshape(nsub, kc, nc2)
-    c_src[:, 0:kc, :] = cres_t.reshape(nsub, kc, nc1)
+    both_t = jnp.concatenate([basis_t, dot(own_rows, basis_t).astype(BF16)], axis=0)
+    ld_resid.wait()
+    for load in loads[8:]:
+        load.start()
+    wide = jnp.concatenate([dofw[...]] * (-(-cols // LANES)), axis=1)[:, :cols]
+    weighted[...] = (wide * resid[...].astype(F32)).astype(BF16)
+    coarse_t = dot(both_t, weighted[...]).T.astype(BF16)
+    t_src[...] = coarse_t[:, nc1:].reshape(nsub, kc, nc2)
+    c_src[:, 0:kc, :] = coarse_t[:, :nc1].reshape(nsub, kc, nc1)
     high = lax.shift_right_logical(cmap[...], 8)
     map_rows = jnp.concatenate(
         [high.astype(F32), (cmap[...] - high * 256).astype(F32), jnp.zeros((kc - 2, nc1), F32)], axis=0
     ).astype(BF16)
     c_src[:, kc : 2 * kc, :] = jnp.broadcast_to(map_rows[None], (nsub, kc, nc1))
-
-    for load in loads[8:]:
-        load.start()
 
     pl.semaphore_wait(barrier, nsub + ngrp - 2)
 
@@ -285,7 +286,6 @@
     c_recv[sub] = c_src[sub]
 
     ld_linv.wait()
-    wide = jnp.concatenate([dofw[...]] * (-(-cols // LANES)), axis=1)[:, :cols]
     scaled[...] = (wide * dot(linv[...], weighted[...])).astype(BF16)
     order_col = jnp.broadcast_to(order.astype(F32), (LANES, n_if)).T.astype(jnp.int32)
 
@@ -458,26 +458,26 @@
         both = jnp.concatenate([xcoef[here, :], xn[f, here, :]], axis=1)
         return (base[rows, here] + dot_t(pair[rows, :], both)).astype(BF16)
 
+    wait_bytes(xn.at[1 - odd], xf_recv.at[0])
+    lower = jnp.concatenate([summed(0, slice(0, cols)), summed(1, slice(0, cols))], axis=0)
+    sol_acc[...] = dot(perm_t[:, 0 : 2 * face], lower).astype(BF16)
+    img_acc[...] = dot(schur_p[:, 0 : 2 * face], lower)
+
     for f in (2, 3):
 
         @pl.when(exists[f])
         def _(f=f):
             wait_bytes(xn.at[f], xz_recv.at[f - 2])
 
-    upper = jnp.concatenate([summed(2, slice(0, cols)), summed(3, slice(0, cols))], axis=0)
-    sol_acc[...] = dot(perm_t[:, 2 * face :], upper).astype(BF16)
-    img_acc[...] = dot(schur_p[:, 2 * face :], upper)
-
-    wait_bytes(xn.at[1 - odd], xf_recv.at[0])
     stores = []
     for h in range(2):
         here = slice(h * half, (h + 1) * half)
-        lower = jnp.concatenate([summed(0, here), summed(1, here)], axis=0)
+        upper = jnp.concatenate([summed(2, here), summed(3, here)], axis=0)
         there = pl.ds(h * half, half)
-        sol[:, here] = (sol_acc[:, here].astype(F32) + dot(perm_t[:, 0 : 2 * face], lower)).astype(BF16)
+        sol[:, here] = (sol_acc[:, here].astype(F32) + dot(perm_t[:, 2 * face :], upper)).astype(BF16)
         stores.append(pltpu.make_async_copy(sol.at[:, there], sol_h.at[0, 0, :, there], out_sem.at[0, h]))
         stores[-1].start()
-        img[:, here] = (img_acc[:, here] + dot(schur_p[:, 0 : 2 * face], lower)).astype(BF16)
+        img[:, here] = (img_acc[:, here] + dot(schur_p[:, 2 * face :], upper)).astype(BF16)
         stores.append(pltpu.make_async_copy(img.at[:, there], img_h.at[0, 0, :, there], out_sem.at[1, h]))
         stores[-1].start()
 

time: 39.9 us -> 38.9 us (0.975)
  Pallas kernels: 39.2 us -> 38.2 us
    pallas_call x1, Pallas kernels: 36.8 us -> 35.8 us  [shards(): pl.pallas_call(functools.partial(kernel, nsub, ngrp), out_shape=(out, out...]
where the time goes in v5:
time: 38.9 us; the launch traced here: 38.8 us
  Pallas kernels  38.2 us (98%)
  between operations  0.64 us (2%)
    pallas_call x1, Pallas kernels, shards(): pl.pallas_call(functools.partial(kernel, nsub, ngrp), out_shape=(out, out...  35.8 us
    pallas_call x1, Pallas kernels, shards(): pl.pallas_call(functools.partial(store, 4), out_shape=(out, out), in_spec...  2.39 us

profile of v5, /device:TPU:1, one launch (start us, length us, event | category | flops | bytes accessed | tf_op | source)
XLA Modules:
  0.0 38.8 jit_solution(430351426177936506)
XLA Ops:
  0.6 35.8 %bddc_apply.1 = (bf16[1,1,1024,512]{3,2,1,0:T(8,128)(2,1)}, bf16[1,1,1024,512]{3,2,1,0:T(8,128)(2,1)}) custom-call(bf16[1,1,1024,512]{3,2,1,0:T(8,128)(2,1)} %resid_h.1, s32[1,1,1024]{2,1,0:T(1,128)} %order_h.1, f32[8,32]{1,0:T(8,128)} %stiff_h.1, bf16[1,1,1024,1024]{3,2,1,0:T(8,128)(2,1)} %schur_h.1, bf16[1,1,1024,1024]{3,2,1,0:T(8,128)(2,1)} %linv_h.1, ...), custom_call_target="tpu_custom_call" | custom-call | flops 6442450944 | bytes 11534336 | tf_op jit(solution)/shard_map/bddc_apply/pallas_call | solution.py:592
  36.4 2.4 %store.1 = (bf16[1,1,1024,512]{3,2,1,0:T(8,128)(2,1)}, bf16[1,1,1024,512]{3,2,1,0:T(8,128)(2,1)}) custom-call(bf16[1,1,1024,512]{3,2,1,0:T(8,128)(2,1)} %get-tuple-element.4.sol, bf16[1,1,1024,512]{3,2,1,0:T(8,128)(2,1)} %get-tuple-element.5.img), custom_call_target="tpu_custom_call" | custom-call | tf_op jit(solution)/shard_map/store/pallas_call | solution.py:604

commit v6 on v5

--- a/solution.py
+++ b/solution.py
@@ -154,11 +154,28 @@
     nx, ny = plane(nsub)
     at_y, at_x, at_c = lax.div(sub, 2 * nx), lax.rem(lax.div(sub, 2), nx), lax.rem(sub, 2)
 
-    def peer_sub(i):
-        j = nsub - 1 - i
-        y = lax.rem(at_y + far_first(lax.div(j, 2 * nx)), ny)
-        x = lax.rem(at_x + far_first(lax.rem(lax.div(j, 2), nx)), nx)
-        return (y * nx + x) * 2 + lax.rem(at_c + lax.rem(j, 2), 2)
+    row = 2 * nx
+    far_x = [lax.rem(at_x + d, nx) * 2 for d in ((2, 3, 1, 0) if nx == 4 else (1, 0))]
+    far_c = [lax.rem(at_c + d, 2) for d in (1, 0)]
+
+    def row_at(r):
+        return lax.rem(at_y + far_first(ny - 1 - r), ny)
+
+    def over_row(y, visit, with_self=False):
+        for i, x in enumerate(far_x):
+            for j, c in enumerate(far_c):
+                t = y * row + x + c
+                if with_self or (i, j) != (nx - 1, 1):
+                    visit(t)
+                else:
+                    pl.when(t != sub)(functools.partial(visit, t))
+
+    def over_plane(visit):
+        def body(r, carry):
+            over_row(row_at(r), visit)
+            return carry
+
+        lax.fori_loop(0, ny, body, 0)
 
     def peer_grp(i):
         off = ngrp // 2 + lax.div(i + 1, 2) * (1 - 2 * lax.rem(i, 2))
@@ -166,15 +183,14 @@
 
     barrier = pltpu.get_barrier_semaphore()
 
-    def greet_sub(i, carry):
-        pl.semaphore_signal(barrier, inc=1, device_id={"sub": peer_sub(i)}, device_id_type=MESH)
-        return carry
+    def greet_sub(t):
+        pl.semaphore_signal(barrier, inc=1, device_id={"sub": t}, device_id_type=MESH)
 
     def greet_grp(i, carry):
         pl.semaphore_signal(barrier, inc=1, device_id={"grp": peer_grp(i)}, device_id_type=MESH)
         return carry
 
-    lax.fori_loop(0, nsub - 1, greet_sub, 0)
+    over_plane(greet_sub)
     lax.fori_loop(0, ngrp - 1, greet_grp, 0)
 
     ld_stiff.wait()
@@ -244,8 +260,7 @@
     def wait_bytes(ref, sem):
         pltpu.make_async_copy(ref, ref, sem).wait()
 
-    def send_t(i, carry):
-        t = peer_sub(i)
+    def send_t(t):
         pltpu.make_async_remote_copy(
             src_ref=t_src.at[t],
             dst_ref=t_recv.at[sub],
@@ -254,10 +269,8 @@
             device_id={"sub": t},
             device_id_type=MESH,
         ).start()
-        return carry
-
-    def send_c(i, carry):
-        t = peer_sub(i)
+
+    def send_c(t):
         pltpu.make_async_remote_copy(
             src_ref=c_src.at[t],
             dst_ref=c_recv.at[sub],
@@ -266,7 +279,6 @@
             device_id={"sub": t},
             device_id_type=MESH,
         ).start()
-        return carry
 
     def send_map3(i, carry):
         pltpu.make_async_remote_copy(
@@ -279,9 +291,9 @@
         ).start()
         return carry
 
-    lax.fori_loop(0, nsub - 1, send_t, 0)
+    over_plane(send_t)
     lax.fori_loop(0, ngrp - 1, send_map3, 0)
-    lax.fori_loop(0, nsub - 1, send_c, 0)
+    over_plane(send_c)
     t_recv[sub] = t_src[sub]
     c_recv[sub] = c_src[sub]
 
@@ -369,49 +381,39 @@
     wait_bytes(recv3.at[:, pl.ds(0, (ngrp - 1) * nc2)], z_sem.at[1])
     picked = two_terms(fold_terms(dot_t(two_terms(recv3[...]), q3[...])))
     sol2 = (local2 + fold_terms(dot(picked, l2basis_t))).astype(BF16)
-    row = 2 * nx
     odd = lax.rem(sub, 2)
 
     def two(t):
         return pl.ds(pl.multiple_of((lax.rem(t, row) + lax.rem(t, 2)) * nc1, nc1), 2 * nc1)
 
     def spread(r, carry):
-        far = ny - 1 - r
-        y = lax.rem(at_y + far_first(far), ny)
+        y = row_at(r)
         here = pl.ds(pl.multiple_of(y * row * nc1, nc1), (row + 2) * nc1)
         back[y] = dot(sol2, onehot2[:, here]).astype(BF16)
 
-        def send_back(i, carry):
-            j = row - 1 - i
-            x = lax.rem(at_x + far_first(lax.div(j, 2)), nx)
-            t = (y * nx + x) * 2 + lax.rem(at_c + lax.rem(j, 2), 2)
-
-            @pl.when(t != sub)
-            def _():
-                pltpu.make_async_remote_copy(
-                    src_ref=back.at[y, :, two(t)],
-                    dst_ref=xtwo.at[block(sub, kc), :],
-                    send_sem=back_sem.at[0],
-                    recv_sem=back_sem.at[1],
-                    device_id={"sub": t},
-                    device_id_type=MESH,
-                ).start()
-
-            return carry
-
-        return lax.fori_loop(0, row, send_back, carry)
+        def send_back(t):
+            pltpu.make_async_remote_copy(
+                src_ref=back.at[y, :, two(t)],
+                dst_ref=xtwo.at[block(sub, kc), :],
+                send_sem=back_sem.at[0],
+                recv_sem=back_sem.at[1],
+                device_id={"sub": t},
+                device_id_type=MESH,
+            ).start()
+
+        over_row(y, send_back)
+        return carry
 
     lax.fori_loop(0, ny, spread, 0)
     xtwo[block(sub, kc), :] = back[at_y, :, two(sub)]
 
-    def send_across(i, carry):
-        t = peer_sub(i)
+    def send_across(r, carry):
+        y = row_at(r)
         for f, step in ((2, -1), (3, 1)):
 
-            @pl.when(exists[f])
-            def _(f=f, step=step):
+            def send(t, f=f, step=step):
                 pltpu.make_async_remote_copy(
-                    src_ref=back.at[lax.div(t, row), :, block(lax.rem(t, row) + 1, nc1)],
+                    src_ref=back.at[y, :, block(t - y * row + 1, nc1)],
                     dst_ref=xn.at[facing[f], block(sub, kc), :],
                     send_sem=xz_send.at[f - 2],
                     recv_sem=xz_recv.at[facing[f] - 2],
@@ -419,9 +421,11 @@
                     device_id_type=MESH,
                 ).start()
 
-        return carry
-
-    lax.fori_loop(0, nsub, send_across, 0)
+            pl.when(exists[f])(functools.partial(over_row, y, send, True))
+
+        return carry
+
+    lax.fori_loop(0, ny, send_across, 0)
 
     ld_schur.wait()
     wide_p = n_if // 2

time: 38.9 us -> 38.1 us (0.979)
  Pallas kernels: 38.2 us -> 37.4 us
    pallas_call x1, Pallas kernels: 35.8 us -> 35 us  [shards(): pl.pallas_call(functools.partial(kernel, nsub, ngrp), out_shape=(out, out...]
where the time goes in v6:
time: 38.1 us; the launch traced here: 38 us
  Pallas kernels  37.4 us (98%)
  between operations  0.64 us (2%)
    pallas_call x1, Pallas kernels, shards(): pl.pallas_call(functools.partial(kernel, nsub, ngrp), out_shape=(out, out...  35 us
    pallas_call x1, Pallas kernels, shards(): pl.pallas_call(functools.partial(store, 4), out_shape=(out, out), in_spec...  2.39 us

profile of v6, /device:TPU:1, one launch (start us, length us, event | category | flops | bytes accessed | tf_op | source)
XLA Modules:
  0.0 38.0 jit_solution(9428165517910478021)
XLA Ops:
  0.6 35.0 %bddc_apply.1 = (bf16[1,1,1024,512]{3,2,1,0:T(8,128)(2,1)}, bf16[1,1,1024,512]{3,2,1,0:T(8,128)(2,1)}) custom-call(bf16[1,1,1024,512]{3,2,1,0:T(8,128)(2,1)} %resid_h.1, s32[1,1,1024]{2,1,0:T(1,128)} %order_h.1, f32[8,32]{1,0:T(8,128)} %stiff_h.1, bf16[1,1,1024,1024]{3,2,1,0:T(8,128)(2,1)} %schur_h.1, bf16[1,1,1024,1024]{3,2,1,0:T(8,128)(2,1)} %linv_h.1, ...), custom_call_target="tpu_custom_call" | custom-call | flops 6442450944 | bytes 11534336 | tf_op jit(solution)/shard_map/bddc_apply/pallas_call | solution.py:596
  35.6 2.4 %store.1 = (bf16[1,1,1024,512]{3,2,1,0:T(8,128)(2,1)}, bf16[1,1,1024,512]{3,2,1,0:T(8,128)(2,1)}) custom-call(bf16[1,1,1024,512]{3,2,1,0:T(8,128)(2,1)} %get-tuple-element.4.sol, bf16[1,1,1024,512]{3,2,1,0:T(8,128)(2,1)} %get-tuple-element.5.img), custom_call_target="tpu_custom_call" | custom-call | tf_op jit(solution)/shard_map/store/pallas_call | solution.py:608

commit v7 on v6

--- a/solution.py
+++ b/solution.py
@@ -326,7 +326,6 @@
     lax.fori_loop(0, ngrp - 1, send_z, 0)
 
     mine_l[...] = dot(perm[...], scaled[...]).astype(BF16)
-    basis_f[...] = dot(perm[...], basis).astype(BF16)
     facing = (1, 0, 3, 2)
 
     def to_neighbour(f, src, dst, send_sem, recv_sem):
@@ -348,7 +347,6 @@
             o = facing[f]
             rows, there = pl.ds(f * face, face), pl.ds(o * face, face)
             to_neighbour(f, mine_l.at[rows], theirs_l.at[there], lf_send.at[f], lf_recv.at[o]).start()
-            to_neighbour(f, basis_f.at[rows], basis_n.at[there], bf_send.at[f], bf_recv.at[o]).start()
 
     wait_bytes(l2maps.at[pl.ds(0, ngrp - 1)], map3_sem.at[1])
 
@@ -426,6 +424,15 @@
         return carry
 
     lax.fori_loop(0, ny, send_across, 0)
+
+    basis_f[...] = dot(perm[...], basis).astype(BF16)
+    for f in (2, 3, 0, 1):
+
+        @pl.when(exists[f])
+        def _(f=f):
+            o = facing[f]
+            rows, there = pl.ds(f * face, face), pl.ds(o * face, face)
+            to_neighbour(f, basis_f.at[rows], basis_n.at[there], bf_send.at[f], bf_recv.at[o]).start()
 
     ld_schur.wait()
     wide_p = n_if // 2

time: 38.1 us -> 38.5 us (1.010)
  no operation moved by 1% of the time
where the time goes in v7:
time: 38.5 us; the launch traced here: 38.1 us
  Pallas kernels  37.4 us (97%)
  between operations  0.64 us (2%)
    pallas_call x1, Pallas kernels, shards(): pl.pallas_call(functools.partial(kernel, nsub, ngrp), out_shape=(out, out...  35 us
    pallas_call x1, Pallas kernels, shards(): pl.pallas_call(functools.partial(store, 4), out_shape=(out, out), in_spec...  2.39 us

profile of v7, /device:TPU:1, one launch (start us, length us, event | category | flops | bytes accessed | tf_op | source)
XLA Modules:
  0.0 38.1 jit_solution(15593764511411752948)
XLA Ops:
  0.6 35.0 %bddc_apply.1 = (bf16[1,1,1024,512]{3,2,1,0:T(8,128)(2,1)}, bf16[1,1,1024,512]{3,2,1,0:T(8,128)(2,1)}) custom-call(bf16[1,1,1024,512]{3,2,1,0:T(8,128)(2,1)} %resid_h.1, s32[1,1,1024]{2,1,0:T(1,128)} %order_h.1, f32[8,32]{1,0:T(8,128)} %stiff_h.1, bf16[1,1,1024,1024]{3,2,1,0:T(8,128)(2,1)} %schur_h.1, bf16[1,1,1024,1024]{3,2,1,0:T(8,128)(2,1)} %linv_h.1, ...), custom_call_target="tpu_custom_call" | custom-call | flops 6442450944 | bytes 11534336 | tf_op jit(solution)/shard_map/bddc_apply/pallas_call | solution.py:603
  35.7 2.4 %store.1 = (bf16[1,1,1024,512]{3,2,1,0:T(8,128)(2,1)}, bf16[1,1,1024,512]{3,2,1,0:T(8,128)(2,1)}) custom-call(bf16[1,1,1024,512]{3,2,1,0:T(8,128)(2,1)} %get-tuple-element.4.sol, bf16[1,1,1024,512]{3,2,1,0:T(8,128)(2,1)} %get-tuple-element.5.img), custom_call_target="tpu_custom_call" | custom-call | tf_op jit(solution)/shard_map/store/pallas_call | solution.py:615
